TPU v7x, 256 devices: a whole 4x4x8 slice. The times are simulated.
256 devices in a mesh: dp: 8 (over x, core), seq: 32 (over y, z).
Axes of the slice: x: 4, y: 4, z: 8, core: 2. Of those that a mesh axis runs over, the one named last changes fastest.
Arguments:
- tokens: bfloat16 [8, 16384, 5120], P('dp', 'seq'), may hold values from -0.059814453 to 0.059814453
- router_weight: float32 [5120], replicated, may hold values from -9 to 9
- routes: int32 [8, 4096], P('dp', 'seq'), may hold values from 0 to 511, as said below
- counts: int32 [8, 32], P('dp', 'seq'), may hold values from 0 to 128, as said below
- query: bfloat16 [8, 4096, 4096], P('dp', 'seq'), may hold values from -120 to 120
- key_in: bfloat16 [8, 4096, 512], P('dp', 'seq'), may hold values from -4 to 4
- value_in: bfloat16 [8, 4096, 512], P('dp', 'seq'), may hold values from -6 to 6
- attn_out: bfloat16 [8, 4096, 4096], P('dp', 'seq'), may hold values from -3 to 3
- grad_out: bfloat16 [8, 4096, 4096], P('dp', 'seq'), may hold values from -6 to 6
Outputs:
- query_grad: bfloat16 [8, 4096, 4096], P('dp', 'seq')
- key_grad: bfloat16 [8, 4096, 512], P('dp', 'seq')
- value_grad: bfloat16 [8, 4096, 512], P('dp', 'seq')
- router_grad: float32 [5120], P(('dp', 'seq'))
Inputs may be any that keep to these rules, and one draw needn't show every extreme that they name: In each sequence the 32 counts sum to 2048; some shard's count is 128. `routes`: entries s * 128 to s * 128 + 127 belong to shard s; those below the shard's count hold distinct token indices of that shard, increasing; the others hold 0.
All inputs are finite; a program needn't handle non-finite values.
Results may differ from a plain program's by a relative error of at most 0.017.
Values may be sent and summed in bfloat16 or wider, within the bound.
A program may use at most 64 MiB of HBM per device.

v0:
```python
import math

import jax
import jax.numpy as jnp
from jax import lax
from jax.sharding import PartitionSpec as P

HEADS = 32
KV = 4
HD = 128


NEGATIVE = -1e30


def attention_grads(queries, key_rows, value_rows, dout_rows, delta_rows, query_pos, key_pos):
    row_count, head_count, head_width = queries.shape
    block_rows = min(512, row_count)
    block_count = row_count // block_rows
    inverse_root = 1.0 / math.sqrt(head_width)

    def block_scores(query_block, key_block):
        query_piece = lax.dynamic_slice_in_dim(queries, query_block * block_rows, block_rows, 0)
        key_piece = lax.dynamic_slice_in_dim(key_rows, key_block * block_rows, block_rows, 0)
        query_place = lax.dynamic_slice_in_dim(query_pos, query_block * block_rows, block_rows, 0)
        key_place = lax.dynamic_slice_in_dim(key_pos, key_block * block_rows, block_rows, 0)
        raw_scores = (
            jnp.einsum("qhe,ke->hqk", query_piece, key_piece, preferred_element_type=jnp.float32)
            * inverse_root
        )
        allowed = key_place[None, None, :] <= query_place[None, :, None]
        return (jnp.where(allowed, raw_scores, NEGATIVE), query_piece, key_piece)

    def row_totals(query_block):

        def row_inner_step(key_block, carry):
            running_max, running_sum = carry
            masked_scores, _, _ = block_scores(query_block, key_block)
            new_max = jnp.maximum(running_max, jnp.max(masked_scores, axis=2))
            running_sum = running_sum * jnp.exp(running_max - new_max) + jnp.sum(
                jnp.exp(masked_scores - new_max[:, :, None]), axis=2
            )
            return (new_max, running_sum)

        start_state = (
            jnp.full((head_count, block_rows), NEGATIVE, jnp.float32),
            jnp.zeros((head_count, block_rows), jnp.float32),
        )
        running_max, running_sum = lax.fori_loop(0, query_block + 1, row_inner_step, start_state)
        return running_max + jnp.log(running_sum)

    log_total = lax.map(row_totals, jnp.arange(block_count, dtype=jnp.int32))

    def key_step(query_grads, key_block):
        value_piece = lax.dynamic_slice_in_dim(value_rows, key_block * block_rows, block_rows, 0)

        def key_inner_step(query_block, carry):
            query_grads, key_sum, value_sum = carry
            masked_scores, query_piece, key_piece = block_scores(query_block, key_block)
            dout_piece = lax.dynamic_slice_in_dim(
                dout_rows, query_block * block_rows, block_rows, 0
            )
            delta_piece = lax.dynamic_slice_in_dim(
                delta_rows, query_block * block_rows, block_rows, 0
            )
            probability = jnp.exp(masked_scores - log_total[query_block][:, :, None])
            value_sum = value_sum + jnp.einsum(
                "hqk,qhe->ke",
                probability.astype(jnp.bfloat16),
                dout_piece,
                preferred_element_type=jnp.float32,
            )
            prob_grad = jnp.einsum(
                "qhe,ke->hqk", dout_piece, value_piece, preferred_element_type=jnp.float32
            )
            score_grad = (
                probability * (prob_grad - delta_piece.T[:, :, None]) * inverse_root
            ).astype(jnp.bfloat16)
            query_piece_grad = jnp.einsum(
                "hqk,ke->qhe", score_grad, key_piece, preferred_element_type=jnp.float32
            )
            previous = lax.dynamic_slice_in_dim(
                query_grads, query_block * block_rows, block_rows, 0
            )
            query_grads = lax.dynamic_update_slice_in_dim(
                query_grads, previous + query_piece_grad, query_block * block_rows, 0
            )
            key_sum = key_sum + jnp.einsum(
                "hqk,qhe->ke", score_grad, query_piece, preferred_element_type=jnp.float32
            )
            return (query_grads, key_sum, value_sum)

        empty_block = jnp.zeros((block_rows, head_width), jnp.float32)
        query_grads, key_sum, value_sum = lax.fori_loop(
            key_block, block_count, key_inner_step, (query_grads, empty_block, empty_block)
        )
        return (query_grads, (key_sum, value_sum))

    query_grads, (key_blocks, value_blocks) = lax.scan(
        key_step,
        jnp.zeros((row_count, head_count, head_width), jnp.float32),
        jnp.arange(block_count, dtype=jnp.int32),
    )
    return (
        query_grads,
        key_blocks.reshape(row_count, head_width),
        value_blocks.reshape(row_count, head_width),
    )


def on_device(tokens, router_weight, routes, counts, query, key_in, value_in, attn_out, grad_out):
    seq_count = lax.axis_size("seq")
    tok_count = tokens.shape[1]
    capacity = routes.shape[1]
    group_size = seq_count // KV
    heads_here = HEADS // seq_count
    slot_routes = routes[0]
    live_slots = jnp.arange(capacity, dtype=jnp.int32) < counts[0, 0]
    picked = jnp.take(tokens[0], slot_routes, axis=0)
    logit = jnp.dot(picked.astype(jnp.float32), router_weight, precision=lax.Precision.HIGHEST)
    gate_value = jax.nn.sigmoid(logit)
    kept_gate = jnp.where(live_slots, gate_value, 0.0)
    cotangent = grad_out[0]
    scaled_cot = (kept_gate[:, None] * cotangent.astype(jnp.float32)).astype(jnp.bfloat16)
    gate_grad = jnp.sum(cotangent.astype(jnp.float32) * attn_out[0].astype(jnp.float32), axis=1)
    logit_grad = jnp.where(live_slots, gate_grad * gate_value * (1.0 - gate_value), 0.0)
    router_part = lax.psum_scatter(
        jnp.dot(logit_grad, picked.astype(jnp.float32), precision=lax.Precision.HIGHEST),
        ("dp", "seq"),
        scatter_dimension=0,
        tiled=True,
    )
    all_routes, all_counts = (
        lax.all_gather(routes, "seq", axis=1, tiled=True),
        lax.all_gather(counts, "seq", axis=1, tiled=True),
    )
    row_count = seq_count * capacity
    slot_index = jnp.arange(row_count, dtype=jnp.int32)
    shard_index = slot_index // capacity
    live_all = slot_index % capacity < jnp.repeat(all_counts[0], capacity)
    position = shard_index * tok_count + all_routes[0]
    seq_tokens = seq_count * tok_count
    query_pos = jnp.where(live_all, position, seq_tokens)
    key_pos = jnp.where(live_all, position, seq_tokens + 1)

    def spread(source):
        return jnp.broadcast_to(
            source[0].reshape(capacity, KV, 1, HD), (capacity, KV, group_size, HD)
        ).reshape(capacity, seq_count * HD)

    head_query, head_key, head_value, head_dout, head_output = (
        lax.all_to_all(query[0], "seq", split_axis=1, concat_axis=0, tiled=True),
        lax.all_to_all(spread(key_in), "seq", split_axis=1, concat_axis=0, tiled=True),
        lax.all_to_all(spread(value_in), "seq", split_axis=1, concat_axis=0, tiled=True),
        lax.all_to_all(scaled_cot, "seq", split_axis=1, concat_axis=0, tiled=True),
        lax.all_to_all(attn_out[0], "seq", split_axis=1, concat_axis=0, tiled=True),
    )
    deltas = jnp.sum(
        (head_dout.astype(jnp.float32) * head_output.astype(jnp.float32)).reshape(
            row_count, heads_here, HD
        ),
        axis=2,
    )
    queries = head_query.reshape(row_count, heads_here, HD)
    douts = head_dout.reshape(row_count, heads_here, HD)
    query_grads, key_grads, value_grads = attention_grads(
        queries, head_key, head_value, douts, deltas, query_pos, key_pos
    )
    key_terms = key_grads.astype(jnp.bfloat16)
    value_terms = value_grads.astype(jnp.bfloat16)
    query_home = lax.all_to_all(
        query_grads.reshape(row_count, heads_here * HD).astype(jnp.bfloat16),
        "seq",
        split_axis=0,
        concat_axis=1,
        tiled=True,
    )
    key_home, value_home = (
        lax.all_to_all(key_terms, "seq", split_axis=0, concat_axis=1, tiled=True),
        lax.all_to_all(value_terms, "seq", split_axis=0, concat_axis=1, tiled=True),
    )

    def fold_heads(piece):
        summed = jnp.sum(piece.astype(jnp.float32).reshape(capacity, KV, group_size, HD), axis=2)
        return summed.reshape(capacity, KV * HD).astype(jnp.bfloat16)

    return (query_home[None], fold_heads(key_home)[None], fold_heads(value_home)[None], router_part)


def solution(mesh):
    placed = (
        P("dp", "seq", None),
        P(),
        P("dp", "seq"),
        P("dp", "seq"),
        P("dp", "seq", None),
        P("dp", "seq", None),
        P("dp", "seq", None),
        P("dp", "seq", None),
        P("dp", "seq", None),
    )
    return jax.shard_map(
        on_device,
        mesh=mesh,
        in_specs=placed,
        out_specs=(
            P("dp", "seq", None),
            P("dp", "seq", None),
            P("dp", "seq", None),
            P(("dp", "seq")),
        ),
        check_vma=False,
    )
```

profile of v0, /device:TPU:6, one launch (start us, length us, event | category | flops | bytes accessed | tf_op | source)
XLA Modules:
  0.0 668.1 jit_solution(5538641322564801188)
XLA Ops:
  2.9 11.5 %all-to-all-start.1 = ((bf16[128,32,128]{2,0,1:T(8,128)(2,1)}), bf16[128,32,128]{2,0,1:T(8,128)(2,1)S(1)}, u32[]{:S(2)}, u32[]{:S(2)}) async-start(bf16[128,32,128]{2,0,1:T(8,128)(2,1)} %bitcast.30), calls=%async_computation.1 | async-start | bytes 2097152 | tf_op jit(solution)/shard_map/all_to_all | solution.py:153
  15.7 27.3 %all-to-all-done.1 = bf16[128,32,128]{2,0,1:T(8,128)(2,1)S(1)} async-done(((bf16[128,32,128]{2,0,1:T(8,128)(2,1)}), bf16[128,32,128]{2,0,1:T(8,128)(2,1)S(1)}, u32[]{:S(2)}, u32[]{:S(2)}) %all-to-all-start.1) | async-done | bytes 1048608 | tf_op jit(solution)/shard_map/all_to_all | solution.py:153
  44.0 5.1 all-to-all-start.4
  50.4 27.0 %all-to-all-done.4 = bf16[128,32,128]{0,2,1:T(8,128)(2,1)S(1)} async-done(((bf16[128,32,128]{0,2,1:T(8,128)(2,1)}), bf16[128,32,128]{0,2,1:T(8,128)(2,1)S(1)}, u32[]{:S(2)}, u32[]{:S(2)}) %all-to-all-start.4) | async-done | bytes 1048608 | tf_op jit(solution)/shard_map/all_to_all | solution.py:156
  77.4 5.0 all-to-all-start.2
  83.8 7.2 %gather_fusion = bf16[128,5120]{1,0:T(8,128)(2,1)} fusion(bf16[512,5120]{1,0:T(8,128)(2,1)} %bitcast.222, s32[1024]{0:T(1024)S(1)} %pad_clamp_fusion), kind=kCustom, calls=%fused_computation | custom fusion | bytes 2621952 | tf_op jit(solution)/shard_map/jit(_take)/gather | solution.py:119
  91.1 2.5 compare_select_fusion.3
  94.9 15.9 %all-to-all-done.2 = bf16[128,32,128]{0,2,1:T(8,128)(2,1)S(1)} async-done(((bf16[128,32,128]{0,2,1:T(8,128)(2,1)}), bf16[128,32,128]{0,2,1:T(8,128)(2,1)S(1)}, u32[]{:S(2)}, u32[]{:S(2)}) %all-to-all-start.2) | async-done | bytes 1048608 | tf_op jit(solution)/shard_map/all_to_all | solution.py:152
  110.8 4.9 all-to-all-start.3
  117.1 37.6 %all-reduce = s32[32]{0:T(128)S(1)} all-reduce(s32[32]{0:T(128)S(1)} %bitcast_dynamic-update-slice_fusion.3), channel_id=1, replica_groups=mesh['dp'=8,'seq'=32] {'seq'}, use_global_device_ids=true, to_apply=%add | all-reduce | flops 32 | bytes 256
  154.6 38.9 %all_gather.7 = s32[1,4096]{1,0:T(1,128)S(1)} all-gather(s32[1,128]{1,0:T(1,128)S(1)} %copy-done.11), channel_id=1, replica_groups=mesh['dp'=8,'seq'=32] {'seq'}, dimensions={1}, use_global_device_ids=true | all-gather | bytes 16896 | tf_op jit(solution)/shard_map/all_gather | solution.py:134
  195.5 7.0 %all-to-all-start = ((bf16[128,32,128]{2,0,1:T(8,128)(2,1)}), bf16[128,32,128]{2,0,1:T(8,128)(2,1)}, u32[]{:S(2)}, u32[]{:S(2)}) async-start(bf16[128,32,128]{2,0,1:T(8,128)(2,1)} %bitcast.27), calls=%async_computation | async-start | bytes 2097152 | tf_op jit(solution)/shard_map/all_to_all | solution.py:154
  202.5 72.8 %while.55 = (s32[]{:T(128)}, f32[8,1,512]{2,1,0:T(1,128)S(1)}, s32[8]{0:T(128)S(1)}, s32[4096]{0:T(1024)S(1)}, bf16[4096,1,128]{2,0,1:T(8,128)(2,1)S(1)}, /*inde...) while((s32[]{:T(128)}, f32[8,1,512]{2,1,0:T(1,128)S(1)}, ...), condition=%wide.region_6.7_spmd, body=%wide.region_1.6_spmd.sunk | while | flops 68683280 | bytes 2671130 | solution.py:52
  208.2 3.1 while.58
  213.4 4.7 while.58
  220.1 6.3 while.58
  228.5 7.8 %while.58 = (s32[]{:T(128)}, f32[1,512]{1,0:T(1,128)S(1)}, f32[1,512]{1,0:T(1,128)S(1)}, s32[]{:T(128)}, s32[4096]{0:T(1024)S(1)}, /*index=5*/s32[512]{0:T(512)S...) while((s32[]{:T(128)}, f32[1,512]{1,0:T(1,128)S(1)}, ...), condition=%wide.region_5.5_spmd, body=%wide.region_2.4_spmd.sunk | while | flops 68682760 | bytes 2394283 | solution.py:49
  238.3 9.4 %while.58 = (s32[]{:T(128)}, f32[1,512]{1,0:T(1,128)S(1)}, f32[1,512]{1,0:T(1,128)S(1)}, s32[]{:T(128)}, s32[4096]{0:T(1024)S(1)}, /*index=5*/s32[512]{0:T(512)S...) while((s32[]{:T(128)}, f32[1,512]{1,0:T(1,128)S(1)}, ...), condition=%wide.region_5.5_spmd, body=%wide.region_2.4_spmd.sunk | while | flops 68682760 | bytes 2394283 | solution.py:49
  249.8 10.9 %while.58 = (s32[]{:T(128)}, f32[1,512]{1,0:T(1,128)S(1)}, f32[1,512]{1,0:T(1,128)S(1)}, s32[]{:T(128)}, s32[4096]{0:T(1024)S(1)}, /*index=5*/s32[512]{0:T(512)S...) while((s32[]{:T(128)}, f32[1,512]{1,0:T(1,128)S(1)}, ...), condition=%wide.region_5.5_spmd, body=%wide.region_2.4_spmd.sunk | while | flops 68682760 | bytes 2394283 | solution.py:49
  262.8 12.5 %while.58 = (s32[]{:T(128)}, f32[1,512]{1,0:T(1,128)S(1)}, f32[1,512]{1,0:T(1,128)S(1)}, s32[]{:T(128)}, s32[4096]{0:T(1024)S(1)}, /*index=5*/s32[512]{0:T(512)S...) while((s32[]{:T(128)}, f32[1,512]{1,0:T(1,128)S(1)}, ...), condition=%wide.region_5.5_spmd, body=%wide.region_2.4_spmd.sunk | while | flops 68682760 | bytes 2394283 | solution.py:49
  279.2 229.7 %while.57 = (s32[]{:T(128)}, f32[4096,1,128]{2,0,1:T(8,128)}, bf16[8,512,128]{2,1,0:T(8,128)(2,1)}, bf16[8,512,128]{2,1,0:T(8,128)(2,1)}, s32[8]{0:T(128)S(1)}, ...) while((s32[]{:T(128)}, f32[4096,1,128]{2,0,1:T(8,128)}, ...), condition=%wide.region_10.11_spmd, body=%wide.region_7.10_spmd.sunk | while | flops 338100224 | bytes 9331396 | solution.py:99
  282.4 43.5 %while.59 = (s32[]{:T(128)}, f32[4096,1,128]{2,0,1:T(8,128)}, f32[512,128]{1,0:T(8,128)S(1)}, f32[512,128]{1,0:T(8,128)S(1)}, s32[512]{0:T(512)S(1)}, /*index=5*...) while((s32[]{:T(128)}, f32[4096,1,128]{2,0,1:T(8,128)}, ...), condition=%wide.region_9.9_spmd, body=%wide.region_8.8_spmd.sunk | while | flops 338100224 | bytes 7229717 | solution.py:94
  285.3 2.0 fusion.91
  296.0 2.0 fusion.91
  301.3 2.0 fusion.91
  306.7 2.0 fusion.91
  317.4 2.0 fusion.91
  322.7 2.0 fusion.91
  329.8 38.1 %while.59 = (s32[]{:T(128)}, f32[4096,1,128]{2,0,1:T(8,128)}, f32[512,128]{1,0:T(8,128)S(1)}, f32[512,128]{1,0:T(8,128)S(1)}, s32[512]{0:T(512)S(1)}, /*index=5*...) while((s32[]{:T(128)}, f32[4096,1,128]{2,0,1:T(8,128)}, ...), condition=%wide.region_9.9_spmd, body=%wide.region_8.8_spmd.sunk | while | flops 338100224 | bytes 7229717 | solution.py:94
  332.7 2.0 fusion.91
  343.4 2.0 fusion.91
  348.7 2.0 fusion.91
  359.4 2.0 fusion.91
  364.8 2.0 fusion.91
  371.9 32.8 %while.59 = (s32[]{:T(128)}, f32[4096,1,128]{2,0,1:T(8,128)}, f32[512,128]{1,0:T(8,128)S(1)}, f32[512,128]{1,0:T(8,128)S(1)}, s32[512]{0:T(512)S(1)}, /*index=5*...) while((s32[]{:T(128)}, f32[4096,1,128]{2,0,1:T(8,128)}, ...), condition=%wide.region_9.9_spmd, body=%wide.region_8.8_spmd.sunk | while | flops 338100224 | bytes 7229717 | solution.py:94
  374.8 2.0 fusion.91
  380.1 2.0 fusion.91
  385.5 2.0 fusion.91
  396.2 2.0 fusion.91
  401.5 2.0 fusion.91
  408.6 27.4 %while.59 = (s32[]{:T(128)}, f32[4096,1,128]{2,0,1:T(8,128)}, f32[512,128]{1,0:T(8,128)S(1)}, f32[512,128]{1,0:T(8,128)S(1)}, s32[512]{0:T(512)S(1)}, /*index=5*...) while((s32[]{:T(128)}, f32[4096,1,128]{2,0,1:T(8,128)}, ...), condition=%wide.region_9.9_spmd, body=%wide.region_8.8_spmd.sunk | while | flops 338100224 | bytes 7229717 | solution.py:94
  411.5 2.0 fusion.91
  416.9 2.0 fusion.91
  427.6 2.0 fusion.91
  432.9 2.0 fusion.91
  440.0 22.1 %while.59 = (s32[]{:T(128)}, f32[4096,1,128]{2,0,1:T(8,128)}, f32[512,128]{1,0:T(8,128)S(1)}, f32[512,128]{1,0:T(8,128)S(1)}, s32[512]{0:T(512)S(1)}, /*index=5*...) while((s32[]{:T(128)}, f32[4096,1,128]{2,0,1:T(8,128)}, ...), condition=%wide.region_9.9_spmd, body=%wide.region_8.8_spmd.sunk | while | flops 338100224 | bytes 7229717 | solution.py:94
  442.9 2.0 fusion.91
  453.6 2.0 fusion.91
  458.9 2.0 fusion.91
  466.0 16.7 %while.59 = (s32[]{:T(128)}, f32[4096,1,128]{2,0,1:T(8,128)}, f32[512,128]{1,0:T(8,128)S(1)}, f32[512,128]{1,0:T(8,128)S(1)}, s32[512]{0:T(512)S(1)}, /*index=5*...) while((s32[]{:T(128)}, f32[4096,1,128]{2,0,1:T(8,128)}, ...), condition=%wide.region_9.9_spmd, body=%wide.region_8.8_spmd.sunk | while | flops 338100224 | bytes 7229717 | solution.py:94
  468.9 2.0 fusion.91
  474.3 2.0 fusion.91
  479.6 2.0 fusion.91
  486.7 11.4 %while.59 = (s32[]{:T(128)}, f32[4096,1,128]{2,0,1:T(8,128)}, f32[512,128]{1,0:T(8,128)S(1)}, f32[512,128]{1,0:T(8,128)S(1)}, s32[512]{0:T(512)S(1)}, /*index=5*...) while((s32[]{:T(128)}, f32[4096,1,128]{2,0,1:T(8,128)}, ...), condition=%wide.region_9.9_spmd, body=%wide.region_8.8_spmd.sunk | while | flops 338100224 | bytes 7229717 | solution.py:94
  489.6 2.0 fusion.91
  495.0 2.0 fusion.91
  502.0 6.0 while.59
  504.9 2.0 fusion.91
  508.8 30.9 %all_to_all.113 = bf16[32,128,128]{2,1,0:T(8,128)(2,1)} all-to-all(bf16[32,128,128]{2,1,0:T(8,128)(2,1)} %bitcast.234), channel_id=1, replica_groups=mesh['dp'=8,'seq'=32] {'seq'}, dimensions={0} | all-to-all | bytes 2097152 | tf_op jit(solution)/shard_map/all_to_all | solution.py:180
  539.7 10.0 %all-to-all-start.6 = ((bf16[32,128,128]{2,1,0:T(8,128)(2,1)}), bf16[32,128,128]{2,1,0:T(8,128)(2,1)}, u32[]{:S(2)}, u32[]{:S(2)}) async-start(bf16[32,128,128]{2,1,0:T(8,128)(2,1)} %bitcast.57), calls=%async_computation.6 | async-start | bytes 2097152 | tf_op jit(solution)/shard_map/all_to_all | solution.py:179
  550.8 24.1 %all-to-all-done.6 = bf16[32,128,128]{2,1,0:T(8,128)(2,1)} async-done(((bf16[32,128,128]{2,1,0:T(8,128)(2,1)}), bf16[32,128,128]{2,1,0:T(8,128)(2,1)}, u32[]{:S(2)}, u32[]{:S(2)}) %all-to-all-start.6) | async-done | bytes 1048608 | tf_op jit(solution)/shard_map/all_to_all | solution.py:179
  574.9 7.4 %all-to-all-start.5 = ((bf16[32,128,128]{2,1,0:T(8,128)(2,1)}), bf16[32,128,128]{2,1,0:T(8,128)(2,1)S(1)}, u32[]{:S(2)}, u32[]{:S(2)}) async-start(bf16[32,128,128]{2,1,0:T(8,128)(2,1)} %bitcast.228), calls=%async_computation.5 | async-start | bytes 2097152 | tf_op jit(solution)/shard_map/all_to_all | solution.py:171
  584.1 2.0 fusion.36
  586.1 76.1 %all-reduce.1 = f32[5120]{0:T(1024)S(1)} all-reduce(f32[5120]{0:T(1024)S(1)} %bitcast.239), channel_id=2, replica_groups=mesh['dp'=8,'seq'=32] {'dp','seq'}, use_global_device_ids=true, to_apply=%region_14.15.clone | all-reduce | flops 5120 | bytes 40960
  (646 shorter events, 180.8 us)
Async XLA Ops:
  0.6 90.4 %copy-start = (f32[5120]{0:T(1024)S(1)}, f32[5120]{0:T(1024)}, u32[]{:S(2)}) copy-start(f32[5120]{0:T(1024)} %param.18) | copy-start | bytes 61444
  0.6 13.8 %copy-start.7 = (bf16[1,128,4096]{2,1,0:T(8,128)(2,1)S(1)}, bf16[1,128,4096]{2,1,0:T(8,128)(2,1)}, u32[]{:S(2)}) copy-start(bf16[1,128,4096]{2,1,0:T(8,128)(2,1)} %param.24) | copy-start | bytes 3145732
  2.9 40.1 %all-to-all-start.1 = ((bf16[128,32,128]{2,0,1:T(8,128)(2,1)}), bf16[128,32,128]{2,0,1:T(8,128)(2,1)S(1)}, u32[]{:S(2)}, u32[]{:S(2)}) async-start(bf16[128,32,128]{2,0,1:T(8,128)(2,1)} %bitcast.30), calls=%async_computation.1 | async-start | bytes 2097152 | tf_op jit(solution)/shard_map/all_to_all | solution.py:153
  14.4 34.7 %copy-start.8 = (bf16[1,128,4096]{2,1,0:T(8,128)(2,1)S(1)}, bf16[1,128,4096]{2,1,0:T(8,128)(2,1)}, u32[]{:S(2)}) copy-start(bf16[1,128,4096]{2,1,0:T(8,128)(2,1)} %param.21) | copy-start | bytes 3145732
  43.1 1.0 copy-start.6
  44.0 33.4 %all-to-all-start.4 = ((bf16[128,32,128]{0,2,1:T(8,128)(2,1)}), bf16[128,32,128]{0,2,1:T(8,128)(2,1)S(1)}, u32[]{:S(2)}, u32[]{:S(2)}) async-start(bf16[128,32,128]{0,2,1:T(8,128)(2,1)} %bitcast.51), calls=%async_computation.4 | async-start | bytes 2097152 | tf_op jit(solution)/shard_map/all_to_all | solution.py:156
  49.1 34.0 %copy-start.9 = (bf16[1,128,4096]{2,1,0:T(8,128)(2,1)S(1)}, bf16[1,128,4096]{2,1,0:T(8,128)(2,1)}, u32[]{:S(2)}) copy-start(bf16[1,128,4096]{2,1,0:T(8,128)(2,1)} %param.25) | copy-start | bytes 3145732
  77.4 5.1 copy-start.4
  77.4 6.4 copy-start.11
  77.4 33.3 %all-to-all-start.2 = ((bf16[128,32,128]{0,2,1:T(8,128)(2,1)}), bf16[128,32,128]{0,2,1:T(8,128)(2,1)S(1)}, u32[]{:S(2)}, u32[]{:S(2)}) async-start(bf16[128,32,128]{0,2,1:T(8,128)(2,1)} %bitcast.37), calls=%async_computation.2 | async-start | bytes 2097152 | tf_op jit(solution)/shard_map/all_to_all | solution.py:152
  83.8 9.8 %copy-start.2 = (bf16[1,128,4096]{1,2,0:T(8,128)(2,1)}, bf16[1,128,4096]{1,2,0:T(8,128)(2,1)S(1)}, u32[]{:S(2)}) copy-start(bf16[1,128,4096]{1,2,0:T(8,128)(2,1)S(1)} %copy.43) | copy-start | bytes 3145732
  93.6 22.1 %copy-start.10 = (bf16[1,128,512]{2,1,0:T(8,128)(2,1)S(1)}, bf16[1,128,512]{2,1,0:T(8,128)(2,1)}, u32[]{:S(2)}) copy-start(bf16[1,128,512]{2,1,0:T(8,128)(2,1)} %param.23) | copy-start | bytes 393220
  93.6 22.2 %copy-start.12 = (u32[256]{0:T(256)S(1)}, u32[256]{0:T(256)}, u32[]{:S(2)}) copy-start(u32[256]{0:T(256)} %constant.175) | copy-start | bytes 3076
  110.8 83.5 %all-to-all-start.3 = ((bf16[128,32,128]{0,2,1:T(8,128)(2,1)}), bf16[128,32,128]{0,2,1:T(8,128)(2,1)S(1)}, u32[]{:S(2)}, u32[]{:S(2)}) async-start(bf16[128,32,128]{0,2,1:T(8,128)(2,1)} %multiply_convert_fusion), calls=%async_computation.3 | async-start | bytes 2097152 | tf_op jit(solution)/shard_map/all_to_all | solution.py:155
  195.5 82.1 %all-to-all-start = ((bf16[128,32,128]{2,0,1:T(8,128)(2,1)}), bf16[128,32,128]{2,0,1:T(8,128)(2,1)}, u32[]{:S(2)}, u32[]{:S(2)}) async-start(bf16[128,32,128]{2,0,1:T(8,128)(2,1)} %bitcast.27), calls=%async_computation | async-start | bytes 2097152 | tf_op jit(solution)/shard_map/all_to_all | solution.py:154
  508.8 40.9 %copy-start.1 = (f32[4096,1,128]{2,0,1:T(8,128)S(1)}, f32[4096,1,128]{2,0,1:T(8,128)}, u32[]{:S(2)}) copy-start(f32[4096,1,128]{2,0,1:T(8,128)} %get-tuple-element.377) | copy-start | bytes 6291460
  539.7 35.2 %all-to-all-start.6 = ((bf16[32,128,128]{2,1,0:T(8,128)(2,1)}), bf16[32,128,128]{2,1,0:T(8,128)(2,1)}, u32[]{:S(2)}, u32[]{:S(2)}) async-start(bf16[32,128,128]{2,1,0:T(8,128)(2,1)} %bitcast.57), calls=%async_computation.6 | async-start | bytes 2097152 | tf_op jit(solution)/shard_map/all_to_all | solution.py:179
  549.7 32.6 %copy-start.3 = (bf16[1,128,4096]{1,2,0:T(8,128)(2,1)S(1)}, bf16[1,128,4096]{1,2,0:T(8,128)(2,1)}, u32[]{:S(2)}) copy-start(bf16[1,128,4096]{1,2,0:T(8,128)(2,1)} %copy-done.2) | copy-start | bytes 3145732
  574.9 91.3 %all-to-all-start.5 = ((bf16[32,128,128]{2,1,0:T(8,128)(2,1)}), bf16[32,128,128]{2,1,0:T(8,128)(2,1)S(1)}, u32[]{:S(2)}, u32[]{:S(2)}) async-start(bf16[32,128,128]{2,1,0:T(8,128)(2,1)} %bitcast.228), calls=%async_computation.5 | async-start | bytes 2097152 | tf_op jit(solution)/shard_map/all_to_all | solution.py:171
  582.2 80.6 %copy-start.5 = (bf16[32,128,128]{2,1,0:T(8,128)(2,1)S(1)}, bf16[32,128,128]{2,1,0:T(8,128)(2,1)}, u32[]{:S(2)}) copy-start(bf16[32,128,128]{2,1,0:T(8,128)(2,1)} %all_to_all.113) | copy-start | bytes 3145732
where the time goes:
time: 674 us; the launch traced here: 668 us
  blocking collectives  183 us (27%)
  matrix products  170 us (25%)
  waiting for transfers between devices  94.2 us (14%)
  loops' own time  90.1 us (13%)
  local copies, waits for them, and re-layouts  61.8 us (9%)
  starting transfers between devices  50.8 us (8%)
  other arithmetic  15.6 us (2%)
    unnamed x2, blocking collectives  114 us
    another operation x8, loops' own time, key_step(): lax.fori_loop(key_block, block_count, key_inner_step, (query_grads, empty...  72.5 us
    dot_general x36, matrix products, key_inner_step(): jnp.einsum('hqk,ke->qhe', score_grad, key_piece, preferred_element_type=j...  70.6 us
    dot_general x72, matrix products, block_scores(): jnp.einsum('qhe,ke->hqk', query_piece, key_piece, preferred_element_type=...  57.9 us
    all_gather x1, blocking collectives, on_device(): lax.all_gather(routes, 'seq', axis=1, tiled=True)  38.9 us
    all_to_all x1, blocking collectives, on_device(): lax.all_to_all(value_terms, 'seq', split_axis=0, concat_axis=1, tiled=True)  30.9 us
    all_to_all x1, waiting for transfers between devices, on_device(): lax.all_to_all(spread(key_in), 'seq', split_axis=1, concat_axis=0, tiled=...  27.3 us
    all_to_all x1, waiting for transfers between devices, on_device(): lax.all_to_all(attn_out[0], 'seq', split_axis=1, concat_axis=0, tiled=True)  27 us
  transfers between devices with their start and end apart: 7, of which 4 were waited for; matrix products, arithmetic and copies ran while one was open for 13% of the time, Pallas kernels for 0%

commit v1 on v0

v1 whole, which is shorter than its diff:
```python
import functools
import math

import jax
import jax.numpy as jnp
from jax import lax
from jax.experimental import pallas as pl
from jax.experimental.pallas import tpu as pltpu
from jax.sharding import PartitionSpec as P

HEADS = 32
KV = 4
HD = 128
GROUP = HEADS // KV
WIDE = GROUP * HD
KEEP = 2048
NEGATIVE = -1e30
MESH = pl.DeviceIdType.MESH
MIB = 1024 * 1024


def place(z_count):
    me = lax.axis_index("seq")
    return me // z_count, me % z_count


def remote(src, dst, send_sem, recv_sem, device):
    return pltpu.make_async_remote_copy(
        src_ref=src,
        dst_ref=dst,
        send_sem=send_sem,
        recv_sem=recv_sem,
        device_id=device,
        device_id_type=MESH,
    )


def greet(devices):
    barrier = pltpu.get_barrier_semaphore()
    for device in devices:
        pl.semaphore_signal(barrier, inc=1, device_id=device, device_id_type=MESH)


def ring_plan(z_count):
    longer = z_count // 2
    shorter = z_count - 1 - longer
    return ((0, 1, longer), (1, -1, longer), (1, 1, shorter), (0, -1, shorter))


def gather_kernel(
    y_count, z_count, chunks,
    tokens, weight, routes, counts, query, key_in, value_in, attn_out, grad_out,
    q_all, do_all, de_all, k_all, v_all, c_all, part,
    tok_v, cot_v, attn_v, dout_v, de_v, cnt_v, picked_v,
    tok_sem, in_sem, own_sem, y_send, y_recv, ring_send, ring_recv, c_send, c_recv,
):
    y, z = place(z_count)
    cap = query.shape[0]
    tok_count = tokens.shape[0]
    chunk = tokens.shape[1] // chunks

    def at(y_there, z_there):
        return {"seq": y_there * z_count + z_there}

    right, left = (z + 1) % z_count, (z + z_count - 1) % z_count
    y_peers = [(y + step) % y_count for step in range(1, y_count)]
    greet([at(other, z) for other in y_peers] + [at(y, right), at(y, left)])

    loads = []
    for c in range(chunks):
        loads.append(pltpu.make_async_copy(tokens.at[:, pl.ds(c * chunk, chunk)], tok_v.at[c], tok_sem.at[c]))
        loads[-1].start()
    rows_in = []
    for g in range(y_count):
        for a, (source, target) in enumerate(((grad_out, cot_v), (attn_out, attn_v))):
            rows_in.append(
                pltpu.make_async_copy(source.at[:, pl.ds(g * WIDE, WIDE)], target.at[g], in_sem.at[a, g])
            )
            rows_in[-1].start()
    cnt_v[...] = jnp.full(cnt_v.shape, counts[0, 0], jnp.int32)

    def wide(ref, g):
        return ref.at[:, pl.ds(pl.multiple_of(g * WIDE, WIDE), WIDE)]

    def narrow(ref, g):
        return ref.at[:, pl.ds(pl.multiple_of(g * HD, HD), HD)]

    own = [
        pltpu.make_async_copy(narrow(key_in, y), k_all.at[z, y], own_sem.at[0]),
        pltpu.make_async_copy(narrow(value_in, y), v_all.at[z, y], own_sem.at[1]),
        pltpu.make_async_copy(cnt_v, c_all.at[z, y], own_sem.at[2]),
        pltpu.make_async_copy(wide(query, y), q_all.at[y], own_sem.at[3]),
    ]
    for copy in own:
        copy.start()
    pl.semaphore_wait(pltpu.get_barrier_semaphore(), y_count + 1)

    first = []
    for i, other in enumerate(y_peers):
        there = at(other, z)
        for a, (source, target) in enumerate(
            (
                (narrow(key_in, other), k_all.at[z, y]),
                (narrow(value_in, other), v_all.at[z, y]),
                (cnt_v, c_all.at[z, y]),
            )
        ):
            first.append(remote(source, target, y_send.at[a, i], y_recv.at[a, i], there))
            first[-1].start()
    late = []
    for i, other in enumerate(y_peers):
        late.append(remote(wide(query, other), q_all.at[y], y_send.at[3, i], y_recv.at[3, i], at(other, z)))
        late[-1].start()
    for copy in own[:3]:
        copy.wait()
    for copy in first:
        copy.wait_recv()

    plan = ring_plan(z_count)
    held = (k_all, v_all)

    def ring_copy(lane, step):
        array, way, _ = plan[lane]
        block = (z - way * step + 2 * z_count) % z_count
        there = at(y, right if way == 1 else left)
        ref = held[array].at[block]
        return remote(ref, ref, ring_send.at[lane, step], ring_recv.at[lane, step], there)

    def count_copy(way, step):
        block = (z - way * step + 2 * z_count) % z_count
        there = at(y, right if way == 1 else left)
        ref = c_all.at[block]
        side = (1 - way) // 2
        return remote(ref, ref, c_send.at[side, step], c_recv.at[side, step], there)

    def forward(step):
        for lane, (array, way, steps) in enumerate(plan):
            if 0 < step <= steps:
                ring_copy(lane, step - 1).wait_recv()
            if step < steps:
                ring_copy(lane, step).start()
            if array == 0:
                if 0 < step <= steps:
                    count_copy(way, step - 1).wait_recv()
                if step < steps:
                    count_copy(way, step).start()

    forward(0)

    token_at = lax.broadcasted_iota(jnp.int32, (tok_count, cap), 0)
    hot = jnp.where(token_at == routes[...], 1.0, 0.0).T.astype(jnp.bfloat16)
    logit = jnp.zeros((cap, HD), jnp.float32)
    for c in range(chunks):
        loads[c].wait()
        picked = jnp.dot(hot, tok_v[c], preferred_element_type=jnp.float32)
        picked_v[c] = picked
        scaled = picked * weight[:, c * chunk : (c + 1) * chunk]
        for t in range(chunk // HD):
            logit = logit + scaled[:, t * HD : (t + 1) * HD]
    logit = jnp.sum(logit, axis=1, keepdims=True)
    gate = 1.0 / (1.0 + jnp.exp(-logit))
    live = lax.broadcasted_iota(jnp.int32, (cap, 1), 0) < counts[0, 0]
    kept = jnp.where(live, gate, 0.0)
    for copy in rows_in:
        copy.wait()

    lane_at = lax.broadcasted_iota(jnp.int32, (cap, HD), 1)

    def scale_group(other):
        gate_sum = jnp.zeros((cap, HD), jnp.float32)
        deltas = jnp.zeros((cap, HD), jnp.float32)
        for h in range(GROUP):
            cols = slice(h * HD, (h + 1) * HD)
            cot = cot_v[other, :, cols].astype(jnp.float32)
            out = attn_v[other, :, cols].astype(jnp.float32)
            dout = (kept * cot).astype(jnp.bfloat16)
            dout_v[other, :, cols] = dout
            gate_sum = gate_sum + cot * out
            delta = jnp.sum(dout.astype(jnp.float32) * out, axis=1, keepdims=True)
            deltas = jnp.where(lane_at == h, delta, deltas)
        de_v[other] = deltas.T[:GROUP]
        return gate_sum

    gate_sum = jnp.zeros((cap, HD), jnp.float32)
    for i, other in enumerate(y_peers):
        gate_sum = gate_sum + scale_group(other)
        for a, (source, target) in enumerate(((dout_v, do_all), (de_v, de_all))):
            late.append(
                remote(source.at[other], target.at[y], y_send.at[4 + a, i], y_recv.at[4 + a, i], at(other, z))
            )
            late[-1].start()
    forward(1)
    gate_sum = gate_sum + scale_group(y)
    mine = [
        pltpu.make_async_copy(dout_v.at[y], do_all.at[y], own_sem.at[4]),
        pltpu.make_async_copy(de_v.at[y], de_all.at[y], own_sem.at[5]),
    ]
    for copy in mine:
        copy.start()
    forward(2)
    gate_grad = jnp.sum(gate_sum, axis=1, keepdims=True)
    logit_grad = jnp.where(live, gate_grad * gate * (1.0 - gate), 0.0)
    segments = part.shape[1]
    for c in range(chunks):
        terms = jnp.sum(logit_grad * picked_v[c], axis=0, keepdims=True)
        for t in range(chunk // HD):
            n = c * (chunk // HD) + t
            part[n // segments, n % segments : n % segments + 1, :] = terms[:, t * HD : (t + 1) * HD]
    for step in range(3, max(p[2] for p in plan) + 1):
        forward(step)
    own[3].wait()
    for copy in mine:
        copy.wait()
    for copy in first:
        copy.wait_send()
    for copy in late:
        copy.wait()
    for lane, (array, way, steps) in enumerate(plan):
        for step in range(steps):
            ring_copy(lane, step).wait_send()
            if array == 0:
                count_copy(way, step).wait_send()


def gather(y_count, z_count, dp_count, tokens, weight, routes, counts, query, key_in, value_in, attn_out, grad_out):
    cap = query.shape[0]
    tok_count, width = tokens.shape
    chunks = 5
    longer = z_count // 2
    anywhere = pl.BlockSpec(memory_space=pl.ANY)
    vmem = pl.BlockSpec(memory_space=pltpu.VMEM)
    smem = pl.BlockSpec(memory_space=pltpu.SMEM)
    bf16, f32 = jnp.bfloat16, jnp.float32
    shape = jax.ShapeDtypeStruct
    return pl.pallas_call(
        functools.partial(gather_kernel, y_count, z_count, chunks),
        out_shape=(
            shape((y_count, cap, WIDE), bf16),
            shape((y_count, cap, WIDE), bf16),
            shape((y_count, GROUP, cap), f32),
            shape((z_count, y_count, cap, HD), bf16),
            shape((z_count, y_count, cap, HD), bf16),
            shape((z_count, y_count, 1, HD), jnp.int32),
            shape((dp_count, width // HD // dp_count, HD), f32),
        ),
        in_specs=[anywhere, vmem, vmem, smem] + [anywhere] * 5,
        out_specs=(anywhere,) * 6 + (vmem,),
        scratch_shapes=[
            pltpu.VMEM((chunks, tok_count, width // chunks), bf16),
            pltpu.VMEM((y_count, cap, WIDE), bf16),
            pltpu.VMEM((y_count, cap, WIDE), bf16),
            pltpu.VMEM((y_count, cap, WIDE), bf16),
            pltpu.VMEM((y_count, GROUP, cap), f32),
            pltpu.VMEM((1, HD), jnp.int32),
            pltpu.VMEM((chunks, cap, width // chunks), f32),
            pltpu.SemaphoreType.DMA((chunks,)),
            pltpu.SemaphoreType.DMA((2, y_count)),
            pltpu.SemaphoreType.DMA((6,)),
            pltpu.SemaphoreType.DMA((6, y_count - 1)),
            pltpu.SemaphoreType.DMA((6, y_count - 1)),
            pltpu.SemaphoreType.DMA((4, longer)),
            pltpu.SemaphoreType.DMA((4, longer)),
            pltpu.SemaphoreType.DMA((2, longer)),
            pltpu.SemaphoreType.DMA((2, longer)),
        ],
        compiler_params=pltpu.CompilerParams(
            collective_id=0, has_side_effects=True, vmem_limit_bytes=40 * MIB
        ),
        name="gather",
    )(tokens, weight, routes, counts, query, key_in, value_in, attn_out, grad_out)


def attention_kernel(
    y_count, z_count, block_rows, block_keys,
    counts, q_in, do_in, de_in, k_in, v_in,
    dq_out, dk_out, dv_out,
    row_f, do_f, de_f, q_b, do_b, de_b, k_f, v_f, k_b, v_b, scores, dk_f, dv_f, dq_f,
):
    cap = q_in.shape[1]
    z = lax.axis_index("seq") % z_count
    shard_count = y_count * z_count
    lanes = GROUP * block_rows
    key_blocks = KEEP // block_keys
    root = 1.0 / math.sqrt(HD)
    power = root * math.log2(math.e)
    f32, bf16 = jnp.float32, jnp.bfloat16

    def pack_keys(shard, offset):
        zz, yy = shard % z_count, shard // z_count
        k_f[pl.ds(offset, cap), :] = k_in[zz, yy].astype(f32)
        v_f[pl.ds(offset, cap), :] = v_in[zz, yy].astype(f32)
        return offset + counts[zz, yy, 0, 0]

    lax.fori_loop(0, shard_count, pack_keys, jnp.int32(0))

    def narrow_keys(b, carry):
        rows = pl.ds(b * block_keys, block_keys)
        k_b[b] = k_f[rows, :].astype(bf16)
        v_b[b] = v_f[rows, :].astype(bf16)
        dk_f[b] = jnp.zeros((block_keys, HD), f32)
        dv_f[b] = jnp.zeros((block_keys, HD), f32)
        return carry

    lax.fori_loop(0, key_blocks, narrow_keys, 0)

    shard_start = []
    total = 0
    for s in range(shard_count):
        shard_start.append(total)
        total = total + counts[s % z_count, s // z_count, 0, 0]

    def key_start(yy):
        picked = jnp.int32(0)
        for zz in range(z_count):
            picked = jnp.where(z == zz, shard_start[yy * z_count + zz], picked)
        return picked

    row_start, shift, live = [], [], []
    rows_here = 0
    for yy in range(y_count):
        row_start.append(rows_here)
        shift.append(key_start(yy) - rows_here)
        live.append(counts[z, yy, 0, 0])
        rows_here = rows_here + live[yy]

    def place_of(row):
        found = row + shift[0]
        for yy in range(1, y_count):
            found = jnp.where(row >= row_start[yy], row + shift[yy], found)
        return found

    for yy in range(y_count):
        rows = pl.ds(row_start[yy], cap)
        for h in range(GROUP):
            cols = slice(h * HD, (h + 1) * HD)
            row_f[h, rows, :] = q_in[yy, :, cols].astype(f32)
            do_f[h, rows, :] = do_in[yy, :, cols].astype(f32)
        padded = jnp.concatenate([de_in[yy], jnp.zeros((HD - GROUP, cap), f32)], axis=0)
        de_f[rows, :] = padded.T
    tail = pl.ds(rows_here, block_rows)
    for h in range(GROUP):
        row_f[h, tail, :] = jnp.zeros((block_rows, HD), f32)
        do_f[h, tail, :] = jnp.zeros((block_rows, HD), f32)
    de_f[tail, :] = jnp.zeros((block_rows, HD), f32)

    row_blocks = (rows_here + block_rows - 1) // block_rows

    def narrow_rows(b, carry):
        rows = pl.ds(pl.multiple_of(b * block_rows, block_rows), block_rows)
        across = de_f[rows, :].T
        for h in range(GROUP):
            mine = slice(h * block_rows, (h + 1) * block_rows)
            q_b[b, mine, :] = row_f[h, rows, :].astype(bf16)
            do_b[b, mine, :] = do_f[h, rows, :].astype(bf16)
            de_b[b, :, mine] = across[h : h + 1, :]
        return carry

    lax.fori_loop(0, row_blocks, narrow_rows, 0)

    nt = (((1,), (1,)), ((), ()))
    tn = (((0,), (0,)), ((), ()))

    def fold(values, combine):
        return combine(values.reshape(block_keys // 8, 8, lanes), axis=0)

    def row_block(b, carry):
        base = b * block_rows
        lane = lax.broadcasted_iota(jnp.int32, (1, lanes), 1)
        row_place = place_of(base + lane % block_rows)
        lowest = place_of(base)
        highest = place_of(jnp.minimum(base + block_rows, rows_here) - 1)
        full = (lowest + 1) // block_keys
        used = highest // block_keys + 1
        queries, douts, delta = q_b[b], do_b[b], de_b[b]

        def score(masked, kb, best):
            block = lax.dot_general(k_b[kb], queries, nt, preferred_element_type=f32)
            if masked:
                key_place = kb * block_keys + lax.broadcasted_iota(jnp.int32, (block_keys, lanes), 0)
                block = jnp.where(key_place <= row_place, block, NEGATIVE)
            scores[kb] = block
            return jnp.maximum(best, fold(block, jnp.max))

        best = jnp.full((8, lanes), NEGATIVE, f32)
        best = lax.fori_loop(0, full, functools.partial(score, False), best)
        best = lax.fori_loop(full, used, functools.partial(score, True), best)
        top = jnp.max(best, axis=0, keepdims=True) * power

        def add_up(kb, total):
            return total + fold(jnp.exp2(scores[kb] * power - top), jnp.sum)

        total = lax.fori_loop(0, used, add_up, jnp.zeros((8, lanes), f32))
        log_total = top + jnp.log2(jnp.sum(total, axis=0, keepdims=True))
        dq_f[:, :] = jnp.zeros(dq_f.shape, f32)

        def grads(kb, carry):
            prob = jnp.exp2(scores[kb] * power - log_total)
            prob_grad = lax.dot_general(v_b[kb], douts, nt, preferred_element_type=f32)
            dv_f[kb] += jnp.dot(prob.astype(bf16), douts, preferred_element_type=f32)
            score_grad = (prob * (prob_grad - delta)).astype(bf16)
            dk_f[kb] += jnp.dot(score_grad, queries, preferred_element_type=f32)
            dq_f[:, :] += lax.dot_general(score_grad, k_b[kb], tn, preferred_element_type=f32)
            return carry

        lax.fori_loop(0, used, grads, 0)
        rows = pl.ds(pl.multiple_of(base, block_rows), block_rows)
        for h in range(GROUP):
            row_f[h, rows, :] = dq_f[h * block_rows : (h + 1) * block_rows, :] * root
        return carry

    lax.fori_loop(0, row_blocks, row_block, 0)

    slot = lax.broadcasted_iota(jnp.int32, (cap, 1), 0)
    for yy in range(y_count):
        rows = pl.ds(row_start[yy], cap)
        for h in range(GROUP):
            grad = jnp.where(slot < live[yy], row_f[h, rows, :], 0.0)
            dq_out[yy, :, h * HD : (h + 1) * HD] = grad.astype(bf16)

    def widen_keys(b, carry):
        rows = pl.ds(pl.multiple_of(b * block_keys, block_keys), block_keys)
        k_f[rows, :] = dk_f[b] * root
        v_f[rows, :] = dv_f[b]
        return carry

    lax.fori_loop(0, key_blocks, widen_keys, 0)

    def unpack_keys(shard, offset):
        zz, yy = shard % z_count, shard // z_count
        count = counts[zz, yy, 0, 0]
        rows = pl.ds(offset, cap)
        dk_out[zz, yy] = jnp.where(slot < count, k_f[rows, :], 0.0).astype(bf16)
        dv_out[zz, yy] = jnp.where(slot < count, v_f[rows, :], 0.0).astype(bf16)
        return offset + count

    lax.fori_loop(0, shard_count, unpack_keys, jnp.int32(0))


def attention(y_count, z_count, counts, q_in, do_in, de_in, k_in, v_in):
    cap = q_in.shape[1]
    block_rows, block_keys = 64, 256
    lanes = GROUP * block_rows
    most = y_count * cap
    row_blocks = most // block_rows
    key_blocks = KEEP // block_keys
    vmem = pl.BlockSpec(memory_space=pltpu.VMEM)
    bf16, f32 = jnp.bfloat16, jnp.float32
    shape = jax.ShapeDtypeStruct
    return pl.pallas_call(
        functools.partial(attention_kernel, y_count, z_count, block_rows, block_keys),
        out_shape=(
            shape((y_count, cap, WIDE), bf16),
            shape((z_count, y_count, cap, HD), bf16),
            shape((z_count, y_count, cap, HD), bf16),
        ),
        in_specs=[pl.BlockSpec(memory_space=pltpu.SMEM)] + [vmem] * 5,
        out_specs=(vmem,) * 3,
        scratch_shapes=[
            pltpu.VMEM((GROUP, most + cap, HD), f32),
            pltpu.VMEM((GROUP, most + cap, HD), f32),
            pltpu.VMEM((most + cap, HD), f32),
            pltpu.VMEM((row_blocks, lanes, HD), bf16),
            pltpu.VMEM((row_blocks, lanes, HD), bf16),
            pltpu.VMEM((row_blocks, 1, lanes), f32),
            pltpu.VMEM((KEEP + cap, HD), f32),
            pltpu.VMEM((KEEP + cap, HD), f32),
            pltpu.VMEM((key_blocks, block_keys, HD), bf16),
            pltpu.VMEM((key_blocks, block_keys, HD), bf16),
            pltpu.VMEM((key_blocks, block_keys, lanes), f32),
            pltpu.VMEM((key_blocks, block_keys, HD), f32),
            pltpu.VMEM((key_blocks, block_keys, HD), f32),
            pltpu.VMEM((lanes, HD), f32),
        ],
        compiler_params=pltpu.CompilerParams(vmem_limit_bytes=48 * MIB),
        name="attention",
    )(counts, q_in, do_in, de_in, k_in, v_in)


def scatter_kernel(
    y_count, z_count, dp_count,
    dq_in, dk_in, dv_in, part,
    dq_out, dk_out, dv_out, router_out,
    held, fin, dp_held, y_held, z_held, dp_sum, y_sum,
    own_sem, q_send, q_recv, ring_send, ring_recv, fin_send, fin_recv, r_send, r_recv,
):
    y, z = place(z_count)
    dp = lax.axis_index("dp")
    f32, bf16 = jnp.float32, jnp.bfloat16

    def at(y_there, z_there):
        return {"seq": y_there * z_count + z_there}

    right, left = (z + 1) % z_count, (z + z_count - 1) % z_count
    y_peers = [(y + step) % y_count for step in range(1, y_count)]
    z_peers = [(z + step) % z_count for step in range(1, z_count)]
    dp_peers = [(dp + step) % dp_count for step in range(1, dp_count)]
    peers = [at(other, z) for other in y_peers] + [at(y, other) for other in z_peers]
    peers += [{"dp": other} for other in dp_peers]
    greet(peers)

    def wide(ref, g):
        return ref.at[:, pl.ds(pl.multiple_of(g * WIDE, WIDE), WIDE)]

    def narrow(ref, g):
        return ref.at[:, pl.ds(pl.multiple_of(g * HD, HD), HD)]

    own = [pltpu.make_async_copy(dq_in.at[y], wide(dq_out, y), own_sem.at[0])]
    own[0].start()
    pl.semaphore_wait(pltpu.get_barrier_semaphore(), len(peers))

    plan = ring_plan(z_count)
    mine = (dk_in, dv_in)

    def ring_copy(lane, step):
        array, way, steps = plan[lane]
        block = (z + way * (steps - step) + z_count) % z_count
        there = at(y, right if way == 1 else left)
        source = mine[array].at[block] if step == 0 else held.at[lane, step - 1]
        return remote(source, held.at[lane, step], ring_send.at[lane, step], ring_recv.at[lane, step], there)

    def forward(step):
        for lane, (array, way, steps) in enumerate(plan):
            if step < steps:
                if step > 0:
                    ring_copy(lane, step - 1).wait_recv()
                    block = (z + way * (steps - step) + z_count) % z_count
                    for g in range(y_count):
                        total = held[lane, step - 1, g].astype(f32) + mine[array][block, g].astype(f32)
                        held[lane, step - 1, g] = total.astype(bf16)
                ring_copy(lane, step).start()

    forward(0)
    sends = []
    for i, other in enumerate(y_peers):
        sends.append(remote(dq_in.at[other], wide(dq_out, y), q_send.at[i], q_recv.at[i], at(other, z)))
        sends[-1].start()

    def share(first, source_of, held_ref, peers_there, me):
        copies = []
        for i, there in enumerate(peers_there):
            copies.append(remote(source_of(i), held_ref.at[me], r_send.at[first + i], r_recv.at[first + i], there))
            copies[-1].start()
        return copies

    over_dp = share(0, lambda i: part.at[dp_peers[i]], dp_held, [{"dp": other} for other in dp_peers], dp)
    forward(1)
    for copy in over_dp:
        copy.wait()
    total = part[dp]
    for other in dp_peers:
        total = total + dp_held[other]
    dp_sum[...] = total
    over_y = share(dp_count - 1, lambda i: dp_sum, y_held, [at(other, z) for other in y_peers], y)
    forward(2)
    for copy in over_y:
        copy.wait()
    for other in y_peers:
        total = total + y_held[other]
    y_sum[...] = total
    over_z = share(
        dp_count + y_count - 2, lambda i: y_sum, z_held, [at(y, other) for other in z_peers], z
    )
    for step in range(3, max(p[2] for p in plan)):
        forward(step)
    for copy in over_z:
        copy.wait()
    for other in z_peers:
        total = total + z_held[other]
    router_out[...] = total

    ends = []
    for array, target in ((0, dk_out), (1, dv_out)):
        lanes = [lane for lane in range(4) if plan[lane][0] == array]
        for lane in lanes:
            ring_copy(lane, plan[lane][2] - 1).wait_recv()
        for g in range(y_count):
            total = mine[array][z, g].astype(f32)
            for lane in lanes:
                total = total + held[lane, plan[lane][2] - 1, g].astype(f32)
            fin[array, g] = total.astype(bf16)
        for i, other in enumerate(y_peers):
            ends.append(
                remote(
                    fin.at[array, other],
                    narrow(target, y),
                    fin_send.at[array, i],
                    fin_recv.at[array, i],
                    at(other, z),
                )
            )
            ends[-1].start()
        own.append(pltpu.make_async_copy(fin.at[array, y], narrow(target, y), own_sem.at[1 + array]))
        own[-1].start()
    for lane, (array, way, steps) in enumerate(plan):
        for step in range(steps):
            ring_copy(lane, step).wait_send()
    for copy in own + sends + ends:
        copy.wait()


def scatter(y_count, z_count, dp_count, dq_in, dk_in, dv_in, part):
    cap = dq_in.shape[1]
    longer = z_count // 2
    small = part.shape[1:]
    anywhere = pl.BlockSpec(memory_space=pl.ANY)
    vmem = pl.BlockSpec(memory_space=pltpu.VMEM)
    bf16, f32 = jnp.bfloat16, jnp.float32
    shape = jax.ShapeDtypeStruct
    router_copies = dp_count + y_count + z_count - 3
    return pl.pallas_call(
        functools.partial(scatter_kernel, y_count, z_count, dp_count),
        out_shape=(
            shape((cap, HEADS * HD), bf16),
            shape((cap, KV * HD), bf16),
            shape((cap, KV * HD), bf16),
            shape(small, f32),
        ),
        in_specs=[anywhere, vmem, vmem, vmem],
        out_specs=(anywhere, anywhere, anywhere, vmem),
        scratch_shapes=[
            pltpu.VMEM((4, longer, y_count, cap, HD), bf16),
            pltpu.VMEM((2, y_count, cap, HD), bf16),
            pltpu.VMEM((dp_count,) + small, f32),
            pltpu.VMEM((y_count,) + small, f32),
            pltpu.VMEM((z_count,) + small, f32),
            pltpu.VMEM(small, f32),
            pltpu.VMEM(small, f32),
            pltpu.SemaphoreType.DMA((3,)),
            pltpu.SemaphoreType.DMA((y_count - 1,)),
            pltpu.SemaphoreType.DMA((y_count - 1,)),
            pltpu.SemaphoreType.DMA((4, longer)),
            pltpu.SemaphoreType.DMA((4, longer)),
            pltpu.SemaphoreType.DMA((2, y_count - 1)),
            pltpu.SemaphoreType.DMA((2, y_count - 1)),
            pltpu.SemaphoreType.DMA((router_copies,)),
            pltpu.SemaphoreType.DMA((router_copies,)),
        ],
        compiler_params=pltpu.CompilerParams(
            collective_id=1, has_side_effects=True, vmem_limit_bytes=32 * MIB
        ),
        name="scatter",
    )(dq_in, dk_in, dv_in, part)


def on_device(tokens, router_weight, routes, counts, query, key_in, value_in, attn_out, grad_out):
    y_count = KV
    z_count = lax.axis_size("seq") // y_count
    dp_count = lax.axis_size("dp")
    width = tokens.shape[2]
    q_all, do_all, de_all, k_all, v_all, c_all, part = gather(
        y_count, z_count, dp_count, tokens[0], router_weight[None], routes, counts,
        query[0], key_in[0], value_in[0], attn_out[0], grad_out[0],
    )
    dq, dk, dv = attention(y_count, z_count, c_all, q_all, do_all, de_all, k_all, v_all)
    dq, dk, dv, router = scatter(y_count, z_count, dp_count, dq, dk, dv, part)
    share = width // (dp_count * y_count * z_count)
    router = lax.dynamic_slice(router.reshape(-1), (lax.axis_index("seq") * share,), (share,))
    return (dq[None], dk[None], dv[None], router)


def solution(mesh):
    rows = P("dp", "seq", None)
    return jax.shard_map(
        on_device,
        mesh=mesh,
        in_specs=(rows, P(), P("dp", "seq"), P("dp", "seq"), rows, rows, rows, rows, rows),
        out_specs=(rows, rows, rows, P(("dp", "seq"))),
        check_vma=False,
    )
```

time: 674 us -> 121 us (0.18)
  blocking collectives: 183 us -> 0 us
  matrix products: 170 us -> 0 us
  Pallas kernels: 0 us -> 104 us
  waiting for transfers between devices: 94.2 us -> 0 us
  loops' own time: 90.1 us -> 0 us
  starting transfers between devices: 50.8 us -> 0 us
  local copies, waits for them, and re-layouts: 61.8 us -> 14.1 us
  other arithmetic: 15.6 us -> 0 us
    dot_general x218 -> x0, matrix products: 170 us -> none  [the longest x36 70.6 us: key_inner_step(): jnp.einsum('hqk,ke->qhe', score_grad, key_piece, preferred_element_type=j...]
    unnamed x2 -> x0, blocking collectives: 114 us -> none
    pallas_call x0 -> x3, Pallas kernels: none -> 104 us  [the longest x1 46.7 us: scatter(): pl.pallas_call(functools.partial(scatter_kernel, y_count, z_count, dp_cou...]
    all_to_all x7 -> x0, waiting for transfers between devices: 94.2 us -> none  [the longest x1 27.3 us: on_device(): lax.all_to_all(spread(key_in), 'seq', split_axis=1, concat_axis=0, tiled=...]
    another operation x18 -> x0, loops' own time: 90.1 us -> none  [the longest x8 72.5 us: key_step(): lax.fori_loop(key_block, block_count, key_inner_step, (query_grads, empty...]
    all_to_all x7 -> x0, starting transfers between devices: 50.8 us -> none  [the longest x1 11.5 us: on_device(): lax.all_to_all(spread(key_in), 'seq', split_axis=1, concat_axis=0, tiled=...]
    all_gather x1 -> x0, blocking collectives: 38.9 us -> none  [on_device(): lax.all_gather(routes, 'seq', axis=1, tiled=True)]
    dynamic_slice x200 -> x1, local copies, waits for them, and re-layouts: 31.9 us -> 0.59 us  [on_device(): lax.dynamic_slice(router.reshape(-1), (lax.axis_index('seq') * share,), (...]
  transfers between devices with their start and end apart: 7 -> 0, of which waited for: 4 -> 0; matrix products, arithmetic and copies ran while one was open for 13% -> 0% of each run, Pallas kernels for 0% -> 0%
where the time goes in v1:
time: 121 us; the launch traced here: 119 us
  Pallas kernels  104 us (86%)
  local copies, waits for them, and re-layouts  14.1 us (12%)
  between operations  1.33 us (1%)
    pallas_call x1, Pallas kernels, scatter(): pl.pallas_call(functools.partial(scatter_kernel, y_count, z_count, dp_cou...  46.7 us
    pallas_call x1, Pallas kernels, gather(): pl.pallas_call(functools.partial(gather_kernel, y_count, z_count, chunks)...  35.9 us
    pallas_call x1, Pallas kernels, attention(): pl.pallas_call(functools.partial(attention_kernel, y_count, z_count, bloc...  21.1 us
    unnamed x23, local copies, waits for them, and re-layouts  13.6 us

profile of v1, /device:TPU:6, one launch (start us, length us, event | category | flops | bytes accessed | tf_op | source)
XLA Modules:
  0.0 119.1 jit_solution(5543240224559255447)
XLA Ops:
  1.3 0.0 copy-start
  1.3 2.5 %copy-done = bf16[1,512,5120]{2,1,0:T(8,128)(2,1)S(1)} copy-done((bf16[1,512,5120]{2,1,0:T(8,128)(2,1)S(1)}, bf16[1,512,5120]{2,1,0:T(8,128)(2,1)}, u32[]{:S(2)}) %copy-start) | copy-done | bytes 5242904
  3.8 0.0 copy-start.3
  3.8 1.2 %copy-done.3 = bf16[1,128,4096]{2,1,0:T(8,128)(2,1)S(1)} copy-done((bf16[1,128,4096]{2,1,0:T(8,128)(2,1)S(1)}, bf16[1,128,4096]{2,1,0:T(8,128)(2,1)}, u32[]{:S(2)}) %copy-start.3) | copy-done | bytes 1048600
  5.0 0.0 copy-start.4
  5.0 1.2 %copy-done.4 = bf16[1,128,4096]{2,1,0:T(8,128)(2,1)S(1)} copy-done((bf16[1,128,4096]{2,1,0:T(8,128)(2,1)S(1)}, bf16[1,128,4096]{2,1,0:T(8,128)(2,1)}, u32[]{:S(2)}) %copy-start.4) | copy-done | bytes 1048600
  6.2 0.0 copy-start.5
  6.2 1.2 %copy-done.5 = bf16[1,128,4096]{2,1,0:T(8,128)(2,1)S(1)} copy-done((bf16[1,128,4096]{2,1,0:T(8,128)(2,1)S(1)}, bf16[1,128,4096]{2,1,0:T(8,128)(2,1)}, u32[]{:S(2)}) %copy-start.5) | copy-done | bytes 1048600
  7.4 0.0 copy-start.6
  7.4 0.9 copy-done.6
  8.3 0.0 copy-start.7
  8.3 0.9 copy-done.7
  9.3 0.0 copy-start.8
  9.3 0.7 copy-done.8
  10.0 0.0 copy-start.9
  10.0 0.7 copy-done.9
  10.6 35.9 %gather.1 = (bf16[4,128,1024]{2,1,0:T(8,128)(2,1)S(1)}, bf16[4,128,1024]{2,1,0:T(8,128)(2,1)S(1)}, f32[4,8,128]{2,1,0:T(8,128)S(1)}, bf16[8,4,128,128]{3,2,1,0:T...) custom-call(bf16[512,5120]{1,0:T(8,128)(2,1)S(1)} %bitcast.11, ...), custom_call_target="tpu_custom_call" | custom-call | tf_op jit(solution)/shard_map/gather/pallas_call | solution.py:235
  46.6 0.0 copy-start.1
  46.6 1.0 copy-done.1
  47.6 0.0 copy-start.2
  47.6 1.0 copy-done.2
  48.5 21.1 %attention.1 = (bf16[4,128,1024]{2,1,0:T(8,128)(2,1)S(1)}, bf16[8,4,128,128]{3,2,1,0:T(8,128)(2,1)S(1)}, bf16[8,4,128,128]{3,2,1,0:T(8,128)(2,1)S(1)}) custom-call(s32[8,4,1,128]{3,2,1,0:T(1,128)S(1)} %get-tuple-element.18.counts, bf16[4,128,1024]{2,1,0:T(8,128)(2,1)S(1)} %get-tuple-element.19.q_in, bf16[4,128,1024]{2,1,0:T(8,128)(2,1)S(1)} %get-tuple-element.20.do_in, ...), custom_call_target="tpu_custom_call" | custom-call | tf_op jit(solution)/shard_map/attention/pallas_call | solution.py:449
  69.6 46.7 %scatter.1 = (bf16[128,4096]{1,0:T(8,128)(2,1)S(1)}, bf16[128,512]{1,0:T(8,128)(2,1)S(1)}, bf16[128,512]{1,0:T(8,128)(2,1)S(1)}, f32[5,128]{1,0:T(8,128)S(1)}) custom-call(bf16[4,128,1024]{2,1,0:T(8,128)(2,1)S(1)} %get-tuple-element.24.dq_in, bf16[8,4,128,128]{3,2,1,0:T(8,128)(2,1)S(1)} %get-tuple-element.25.dk_in, ...), custom_call_target="tpu_custom_call" | custom-call | tf_op jit(solution)/shard_map/scatter/pallas_call | solution.py:610
  116.3 0.6 dynamic_slice.3
  116.9 1.0 copy.17
  117.8 0.7 copy.18
  118.5 0.7 copy.19
Async XLA Ops:
  1.3 2.5 %copy-start = (bf16[1,512,5120]{2,1,0:T(8,128)(2,1)S(1)}, bf16[1,512,5120]{2,1,0:T(8,128)(2,1)}, u32[]{:S(2)}) copy-start(bf16[1,512,5120]{2,1,0:T(8,128)(2,1)} %param.9) | copy-start | bytes 15728644
  3.8 1.2 %copy-start.3 = (bf16[1,128,4096]{2,1,0:T(8,128)(2,1)S(1)}, bf16[1,128,4096]{2,1,0:T(8,128)(2,1)}, u32[]{:S(2)}) copy-start(bf16[1,128,4096]{2,1,0:T(8,128)(2,1)} %param.13) | copy-start | bytes 3145732
  5.0 1.2 %copy-start.4 = (bf16[1,128,4096]{2,1,0:T(8,128)(2,1)S(1)}, bf16[1,128,4096]{2,1,0:T(8,128)(2,1)}, u32[]{:S(2)}) copy-start(bf16[1,128,4096]{2,1,0:T(8,128)(2,1)} %param.16) | copy-start | bytes 3145732
  6.2 1.2 %copy-start.5 = (bf16[1,128,4096]{2,1,0:T(8,128)(2,1)S(1)}, bf16[1,128,4096]{2,1,0:T(8,128)(2,1)}, u32[]{:S(2)}) copy-start(bf16[1,128,4096]{2,1,0:T(8,128)(2,1)} %param.17) | copy-start | bytes 3145732
  7.4 0.9 copy-start.6
  8.3 0.9 copy-start.7
  9.3 0.7 copy-start.8
  10.0 0.7 copy-start.9
  46.6 1.0 copy-start.1
  47.6 1.0 copy-start.2

commit v2 on v1

--- a/solution.py
+++ b/solution.py
@@ -14,6 +14,7 @@
 GROUP = HEADS // KV
 WIDE = GROUP * HD
 KEEP = 2048
+SUB_LANES = 128
 NEGATIVE = -1e30
 MESH = pl.DeviceIdType.MESH
 MIB = 1024 * 1024
@@ -264,7 +265,7 @@
             pltpu.SemaphoreType.DMA((2, longer)),
         ],
         compiler_params=pltpu.CompilerParams(
-            collective_id=0, has_side_effects=True, vmem_limit_bytes=40 * MIB
+            collective_id=0, has_side_effects=True, vmem_limit_bytes=63 * MIB
         ),
         name="gather",
     )(tokens, weight, routes, counts, query, key_in, value_in, attn_out, grad_out)
@@ -274,7 +275,8 @@
     y_count, z_count, block_rows, block_keys,
     counts, q_in, do_in, de_in, k_in, v_in,
     dq_out, dk_out, dv_out,
-    row_f, do_f, de_f, q_b, do_b, de_b, k_f, v_f, k_b, v_b, scores, dk_f, dv_f, dq_f,
+    row_f, do_f, de_f, q_b, do_b, de_b, k_f, v_f, k_b, kt_b, v_b, exps, tops, best, total, dk_f, dv_f, dq_f,
+    s_even, s_odd, p_even, p_odd, ds_even, ds_odd, pair_row, pair_key, shard_start,
 ):
     cap = q_in.shape[1]
     z = lax.axis_index("seq") % z_count
@@ -284,42 +286,44 @@
     root = 1.0 / math.sqrt(HD)
     power = root * math.log2(math.e)
     f32, bf16 = jnp.float32, jnp.bfloat16
-
-    def pack_keys(shard, offset):
-        zz, yy = shard % z_count, shard // z_count
-        k_f[pl.ds(offset, cap), :] = k_in[zz, yy].astype(f32)
-        v_f[pl.ds(offset, cap), :] = v_in[zz, yy].astype(f32)
-        return offset + counts[zz, yy, 0, 0]
-
-    lax.fori_loop(0, shard_count, pack_keys, jnp.int32(0))
+    s_b, p_b, ds_b = (s_even, s_odd), (p_even, p_odd), (ds_even, ds_odd)
+
+    def count_of(shard):
+        return counts[shard % z_count, shard // z_count, 0, 0]
+
+    def add_counts(shard, offset):
+        shard_start[shard] = offset
+        return offset + count_of(shard)
+
+    lax.fori_loop(0, shard_count, add_counts, jnp.int32(0))
+
+    def pack_keys(step, carry):
+        for more in range(4):
+            shard = step * 4 + more
+            zz, yy = shard % z_count, shard // z_count
+            rows = pl.ds(shard_start[shard], cap)
+            k_f[rows, :] = k_in[zz, yy].astype(f32)
+            v_f[rows, :] = v_in[zz, yy].astype(f32)
+        return carry
+
+    lax.fori_loop(0, shard_count // 4, pack_keys, 0)
 
     def narrow_keys(b, carry):
         rows = pl.ds(b * block_keys, block_keys)
         k_b[b] = k_f[rows, :].astype(bf16)
+        kt_b[b] = k_f[rows, :].T.astype(bf16)
         v_b[b] = v_f[rows, :].astype(bf16)
         dk_f[b] = jnp.zeros((block_keys, HD), f32)
         dv_f[b] = jnp.zeros((block_keys, HD), f32)
         return carry
 
     lax.fori_loop(0, key_blocks, narrow_keys, 0)
-
-    shard_start = []
-    total = 0
-    for s in range(shard_count):
-        shard_start.append(total)
-        total = total + counts[s % z_count, s // z_count, 0, 0]
-
-    def key_start(yy):
-        picked = jnp.int32(0)
-        for zz in range(z_count):
-            picked = jnp.where(z == zz, shard_start[yy * z_count + zz], picked)
-        return picked
 
     row_start, shift, live = [], [], []
     rows_here = 0
     for yy in range(y_count):
         row_start.append(rows_here)
-        shift.append(key_start(yy) - rows_here)
+        shift.append(shard_start[yy * z_count + z] - rows_here)
         live.append(counts[z, yy, 0, 0])
         rows_here = rows_here + live[yy]
 
@@ -358,57 +362,121 @@
     lax.fori_loop(0, row_blocks, narrow_rows, 0)
 
     nt = (((1,), (1,)), ((), ()))
-    tn = (((0,), (0,)), ((), ()))
-
-    def fold(values, combine):
-        return combine(values.reshape(block_keys // 8, 8, lanes), axis=0)
-
-    def row_block(b, carry):
-        base = b * block_rows
-        lane = lax.broadcasted_iota(jnp.int32, (1, lanes), 1)
-        row_place = place_of(base + lane % block_rows)
-        lowest = place_of(base)
-        highest = place_of(jnp.minimum(base + block_rows, rows_here) - 1)
-        full = (lowest + 1) // block_keys
-        used = highest // block_keys + 1
-        queries, douts, delta = q_b[b], do_b[b], de_b[b]
-
-        def score(masked, kb, best):
-            block = lax.dot_general(k_b[kb], queries, nt, preferred_element_type=f32)
+
+    def list_pairs(masked, count):
+        def of_rows(b, count):
+            full = (place_of(b * block_rows) + 1) // block_keys
+            used = place_of(jnp.minimum((b + 1) * block_rows, rows_here) - 1) // block_keys + 1
+
+            def add(kb, count):
+                pair_row[count] = b
+                pair_key[count] = kb
+                return count + 1
+
+            first, last = (full, used) if masked else (0, full)
+            return lax.fori_loop(first, last, add, count)
+
+        return lax.fori_loop(0, row_blocks, of_rows, count)
+
+    whole_pairs = list_pairs(False, jnp.int32(0))
+    pairs = list_pairs(True, whole_pairs)
+    for more in range(3):
+        pair_row[pairs + more] = q_b.shape[0] - 1
+        pair_key[pairs + more] = 0
+
+    def start_rows(b, carry):
+        best[b] = jnp.full((8, lanes), NEGATIVE, f32)
+        total[b] = jnp.zeros((8, lanes), f32)
+        dq_f[b] = jnp.zeros((HD, lanes), f32)
+        return carry
+
+    lax.fori_loop(0, row_blocks, start_rows, 0)
+
+    def raw(n, slot):
+        s_b[slot][:, :] = lax.dot_general(
+            k_b[pair_key[n]], q_b[pair_row[n]], nt, preferred_element_type=f32
+        )
+
+    def grow(masked, n, slot):
+        b, kb = pair_row[n], pair_key[n]
+        for part in range(lanes // SUB_LANES):
+            cols = slice(part * SUB_LANES, (part + 1) * SUB_LANES)
+            block = s_b[slot][:, cols] * power
             if masked:
-                key_place = kb * block_keys + lax.broadcasted_iota(jnp.int32, (block_keys, lanes), 0)
+                lane = lax.broadcasted_iota(jnp.int32, (1, SUB_LANES), 1)
+                row_place = place_of(b * block_rows + lane % block_rows) - kb * block_keys
+                key_place = lax.broadcasted_iota(jnp.int32, (block_keys, SUB_LANES), 0)
                 block = jnp.where(key_place <= row_place, block, NEGATIVE)
-            scores[kb] = block
-            return jnp.maximum(best, fold(block, jnp.max))
-
-        best = jnp.full((8, lanes), NEGATIVE, f32)
-        best = lax.fori_loop(0, full, functools.partial(score, False), best)
-        best = lax.fori_loop(full, used, functools.partial(score, True), best)
-        top = jnp.max(best, axis=0, keepdims=True) * power
-
-        def add_up(kb, total):
-            return total + fold(jnp.exp2(scores[kb] * power - top), jnp.sum)
-
-        total = lax.fori_loop(0, used, add_up, jnp.zeros((8, lanes), f32))
-        log_total = top + jnp.log2(jnp.sum(total, axis=0, keepdims=True))
-        dq_f[:, :] = jnp.zeros(dq_f.shape, f32)
-
-        def grads(kb, carry):
-            prob = jnp.exp2(scores[kb] * power - log_total)
-            prob_grad = lax.dot_general(v_b[kb], douts, nt, preferred_element_type=f32)
-            dv_f[kb] += jnp.dot(prob.astype(bf16), douts, preferred_element_type=f32)
-            score_grad = (prob * (prob_grad - delta)).astype(bf16)
-            dk_f[kb] += jnp.dot(score_grad, queries, preferred_element_type=f32)
-            dq_f[:, :] += lax.dot_general(score_grad, k_b[kb], tn, preferred_element_type=f32)
-            return carry
-
-        lax.fori_loop(0, used, grads, 0)
-        rows = pl.ds(pl.multiple_of(base, block_rows), block_rows)
+            block = block.reshape(block_keys // 8, 8, SUB_LANES)
+            before = best[b, :, cols]
+            after = jnp.maximum(before, jnp.max(block, axis=0))
+            grown = jnp.exp2(block - after)
+            exps[n, :, :, cols] = grown
+            tops[n, :, cols] = after
+            best[b, :, cols] = after
+            total[b, :, cols] = total[b, :, cols] * jnp.exp2(before - after) + jnp.sum(grown, axis=0)
+
+    def two_scores(masked, j, carry):
+        n = 2 * j
+        raw(n + 1, 1)
+        grow(masked, n, 0)
+        raw(n + 2, 0)
+        grow(masked, n + 1, 1)
+        return carry
+
+    raw(0, 0)
+    lax.fori_loop(0, whole_pairs // 2, functools.partial(two_scores, False), 0)
+    lax.fori_loop(whole_pairs // 2, (pairs + 1) // 2, functools.partial(two_scores, True), 0)
+
+    def finish_rows(b, carry):
+        top = jnp.max(best[b], axis=0, keepdims=True)
+        summed = jnp.sum(total[b] * jnp.exp2(best[b] - top), axis=0, keepdims=True)
+        best[b] = jnp.broadcast_to(top + jnp.log2(summed), (8, lanes))
+        return carry
+
+    lax.fori_loop(0, row_blocks, finish_rows, 0)
+
+    def terms(n, slot):
+        b, kb = pair_row[n], pair_key[n]
+        scale = jnp.exp2(tops[n] - best[b])
+        prob = (exps[n] * scale).reshape(block_keys, lanes)
+        prob_grad = lax.dot_general(v_b[kb], do_b[b], nt, preferred_element_type=f32)
+        p_b[slot][:, :] = prob.astype(bf16)
+        ds_b[slot][:, :] = (prob * (prob_grad - de_b[b])).astype(bf16)
+
+    def products(n, slot):
+        b, kb = pair_row[n], pair_key[n]
+        score_grad = ds_b[slot][:, :]
+        dv_f[kb] += jnp.dot(p_b[slot][:, :], do_b[b], preferred_element_type=f32)
+        dk_f[kb] += jnp.dot(score_grad, q_b[b], preferred_element_type=f32)
+        dq_f[b] += jnp.dot(kt_b[kb], score_grad, preferred_element_type=f32)
+
+    def two_pairs(j, carry):
+        n = 2 * j
+        products(n, 0)
+        terms(n + 1, 1)
+        products(n + 1, 1)
+        terms(n + 2, 0)
+        return carry
+
+    @pl.when(pairs > 0)
+    def _():
+        terms(0, 0)
+
+    lax.fori_loop(0, pairs // 2, two_pairs, 0)
+
+    @pl.when(pairs % 2 == 1)
+    def _():
+        products(pairs - 1, 0)
+
+    def turn_rows(b, carry):
+        rows = pl.ds(pl.multiple_of(b * block_rows, block_rows), block_rows)
+        turned = dq_f[b].T * root
         for h in range(GROUP):
-            row_f[h, rows, :] = dq_f[h * block_rows : (h + 1) * block_rows, :] * root
-        return carry
-
-    lax.fori_loop(0, row_blocks, row_block, 0)
+            row_f[h, rows, :] = turned[h * block_rows : (h + 1) * block_rows, :]
+        return carry
+
+    lax.fori_loop(0, row_blocks, turn_rows, 0)
 
     slot = lax.broadcasted_iota(jnp.int32, (cap, 1), 0)
     for yy in range(y_count):
@@ -425,15 +493,17 @@
 
     lax.fori_loop(0, key_blocks, widen_keys, 0)
 
-    def unpack_keys(shard, offset):
-        zz, yy = shard % z_count, shard // z_count
-        count = counts[zz, yy, 0, 0]
-        rows = pl.ds(offset, cap)
-        dk_out[zz, yy] = jnp.where(slot < count, k_f[rows, :], 0.0).astype(bf16)
-        dv_out[zz, yy] = jnp.where(slot < count, v_f[rows, :], 0.0).astype(bf16)
-        return offset + count
-
-    lax.fori_loop(0, shard_count, unpack_keys, jnp.int32(0))
+    def unpack_keys(step, carry):
+        for more in range(4):
+            shard = step * 4 + more
+            zz, yy = shard % z_count, shard // z_count
+            rows = pl.ds(shard_start[shard], cap)
+            held = slot < count_of(shard)
+            dk_out[zz, yy] = jnp.where(held, k_f[rows, :], 0.0).astype(bf16)
+            dv_out[zz, yy] = jnp.where(held, v_f[rows, :], 0.0).astype(bf16)
+        return carry
+
+    lax.fori_loop(0, shard_count // 4, unpack_keys, 0)
 
 
 def attention(y_count, z_count, counts, q_in, do_in, de_in, k_in, v_in):
@@ -459,19 +529,32 @@
             pltpu.VMEM((GROUP, most + cap, HD), f32),
             pltpu.VMEM((GROUP, most + cap, HD), f32),
             pltpu.VMEM((most + cap, HD), f32),
-            pltpu.VMEM((row_blocks, lanes, HD), bf16),
-            pltpu.VMEM((row_blocks, lanes, HD), bf16),
-            pltpu.VMEM((row_blocks, 1, lanes), f32),
+            pltpu.VMEM((row_blocks + 1, lanes, HD), bf16),
+            pltpu.VMEM((row_blocks + 1, lanes, HD), bf16),
+            pltpu.VMEM((row_blocks + 1, 1, lanes), f32),
             pltpu.VMEM((KEEP + cap, HD), f32),
             pltpu.VMEM((KEEP + cap, HD), f32),
             pltpu.VMEM((key_blocks, block_keys, HD), bf16),
+            pltpu.VMEM((key_blocks, HD, block_keys), bf16),
             pltpu.VMEM((key_blocks, block_keys, HD), bf16),
-            pltpu.VMEM((key_blocks, block_keys, lanes), f32),
+            pltpu.VMEM((row_blocks * key_blocks + 1, block_keys // 8, 8, lanes), f32),
+            pltpu.VMEM((row_blocks * key_blocks + 1, 8, lanes), f32),
+            pltpu.VMEM((row_blocks + 1, 8, lanes), f32),
+            pltpu.VMEM((row_blocks + 1, 8, lanes), f32),
             pltpu.VMEM((key_blocks, block_keys, HD), f32),
             pltpu.VMEM((key_blocks, block_keys, HD), f32),
-            pltpu.VMEM((lanes, HD), f32),
+            pltpu.VMEM((row_blocks, HD, lanes), f32),
+            pltpu.VMEM((block_keys, lanes), f32),
+            pltpu.VMEM((block_keys, lanes), f32),
+            pltpu.VMEM((block_keys, lanes), bf16),
+            pltpu.VMEM((block_keys, lanes), bf16),
+            pltpu.VMEM((block_keys, lanes), bf16),
+            pltpu.VMEM((block_keys, lanes), bf16),
+            pltpu.SMEM((row_blocks * key_blocks + 3,), jnp.int32),
+            pltpu.SMEM((row_blocks * key_blocks + 3,), jnp.int32),
+            pltpu.SMEM((y_count * z_count,), jnp.int32),
         ],
-        compiler_params=pltpu.CompilerParams(vmem_limit_bytes=48 * MIB),
+        compiler_params=pltpu.CompilerParams(vmem_limit_bytes=62 * MIB),
         name="attention",
     )(counts, q_in, do_in, de_in, k_in, v_in)
 

time: 121 us -> 111 us (0.917)
  local copies, waits for them, and re-layouts: 14.1 us -> 7.3 us
  Pallas kernels: 104 us -> 100 us
    pallas_call x1, Pallas kernels: 46.7 us -> 38.6 us  [scatter(): pl.pallas_call(functools.partial(scatter_kernel, y_count, z_count, dp_cou...]
    unnamed x23 -> x11, local copies, waits for them, and re-layouts: 13.6 us -> 6.71 us
    pallas_call x1, Pallas kernels: 21.1 us -> 23.8 us  [attention(): pl.pallas_call(functools.partial(attention_kernel, y_count, z_count, bloc...]
    pallas_call x1, Pallas kernels: 35.9 us -> 37.7 us  [gather(): pl.pallas_call(functools.partial(gather_kernel, y_count, z_count, chunks)...]
where the time goes in v2:
time: 111 us; the launch traced here: 109 us
  Pallas kernels  100 us (90%)
  local copies, waits for them, and re-layouts  7.3 us (7%)
  between operations  1.31 us (1%)
    pallas_call x1, Pallas kernels, scatter(): pl.pallas_call(functools.partial(scatter_kernel, y_count, z_count, dp_cou...  38.6 us
    pallas_call x1, Pallas kernels, gather(): pl.pallas_call(functools.partial(gather_kernel, y_count, z_count, chunks)...  37.7 us
    pallas_call x1, Pallas kernels, attention(): pl.pallas_call(functools.partial(attention_kernel, y_count, z_count, bloc...  23.8 us
    unnamed x11, local copies, waits for them, and re-layouts  6.71 us

profile of v2, /device:TPU:6, one launch (start us, length us, event | category | flops | bytes accessed | tf_op | source)
XLA Modules:
  0.0 108.8 jit_solution(13070403295055138538)
XLA Ops:
  1.3 37.7 %gather.1 = (bf16[4,128,1024]{2,1,0:T(8,128)(2,1)}, bf16[4,128,1024]{2,1,0:T(8,128)(2,1)}, f32[4,8,128]{2,1,0:T(8,128)}, bf16[8,4,128,128]{3,2,1,0:T(8,128)(2,1)...) custom-call(bf16[512,5120]{1,0:T(8,128)(2,1)} %bitcast.15, ...), custom_call_target="tpu_custom_call" | custom-call | tf_op jit(solution)/shard_map/gather/pallas_call | solution.py:236
  39.0 23.8 %attention.1 = (bf16[4,128,1024]{2,1,0:T(8,128)(2,1)}, bf16[8,4,128,128]{3,2,1,0:T(8,128)(2,1)}, bf16[8,4,128,128]{3,2,1,0:T(8,128)(2,1)}) custom-call(s32[8,4,1,128]{3,2,1,0:T(1,128)} %get-tuple-element.18.counts, bf16[4,128,1024]{2,1,0:T(8,128)(2,1)} %get-tuple-element.19.q_in, bf16[4,128,1024]{2,1,0:T(8,128)(2,1)} %get-tuple-element.20.do_in, ...), custom_call_target="tpu_custom_call" | custom-call | tf_op jit(solution)/shard_map/attention/pallas_call | solution.py:519
  62.8 0.0 copy-start
  62.8 1.2 %copy-done = bf16[4,128,1024]{2,1,0:T(8,128)(2,1)S(1)} copy-done((bf16[4,128,1024]{2,1,0:T(8,128)(2,1)S(1)}, bf16[4,128,1024]{2,1,0:T(8,128)(2,1)}, u32[]{:S(2)}) %copy-start) | copy-done | bytes 1048600
  64.0 0.0 copy-start.1
  64.0 1.2 %copy-done.1 = bf16[8,4,128,128]{3,2,1,0:T(8,128)(2,1)S(1)} copy-done((bf16[8,4,128,128]{3,2,1,0:T(8,128)(2,1)S(1)}, bf16[8,4,128,128]{3,2,1,0:T(8,128)(2,1)}, u32[]{:S(2)}) %copy-start.1) | copy-done | bytes 1048600
  65.3 0.0 copy-start.2
  65.3 1.2 %copy-done.2 = bf16[8,4,128,128]{3,2,1,0:T(8,128)(2,1)S(1)} copy-done((bf16[8,4,128,128]{3,2,1,0:T(8,128)(2,1)S(1)}, bf16[8,4,128,128]{3,2,1,0:T(8,128)(2,1)}, u32[]{:S(2)}) %copy-start.2) | copy-done | bytes 1048600
  66.5 0.0 copy-start.3
  66.5 0.8 copy-done.3
  67.3 38.6 %scatter.1 = (bf16[128,4096]{1,0:T(8,128)(2,1)S(1)}, bf16[128,512]{1,0:T(8,128)(2,1)S(1)}, bf16[128,512]{1,0:T(8,128)(2,1)S(1)}, f32[5,128]{1,0:T(8,128)S(1)}) custom-call(bf16[4,128,1024]{2,1,0:T(8,128)(2,1)S(1)} %copy-done, bf16[8,4,128,128]{3,2,1,0:T(8,128)(2,1)S(1)} %copy-done.1, bf16[8,4,128,128]{3,2,1,0:T(8,128)(2,1)S(1)} %copy-done.2, ...), custom_call_target="tpu_custom_call" | custom-call | tf_op jit(solution)/shard_map/scatter/pallas_call | solution.py:693
  105.9 0.6 dynamic_slice.3
  106.5 1.0 copy.17
  107.5 0.7 copy.18
  108.1 0.7 copy.19
Async XLA Ops:
  62.8 1.2 %copy-start = (bf16[4,128,1024]{2,1,0:T(8,128)(2,1)S(1)}, bf16[4,128,1024]{2,1,0:T(8,128)(2,1)}, u32[]{:S(2)}) copy-start(bf16[4,128,1024]{2,1,0:T(8,128)(2,1)} %get-tuple-element.24.dq_in) | copy-start | bytes 3145732
  64.0 1.2 %copy-start.1 = (bf16[8,4,128,128]{3,2,1,0:T(8,128)(2,1)S(1)}, bf16[8,4,128,128]{3,2,1,0:T(8,128)(2,1)}, u32[]{:S(2)}) copy-start(bf16[8,4,128,128]{3,2,1,0:T(8,128)(2,1)} %get-tuple-element.25.dk_in) | copy-start | bytes 3145732
  65.3 1.2 %copy-start.2 = (bf16[8,4,128,128]{3,2,1,0:T(8,128)(2,1)S(1)}, bf16[8,4,128,128]{3,2,1,0:T(8,128)(2,1)}, u32[]{:S(2)}) copy-start(bf16[8,4,128,128]{3,2,1,0:T(8,128)(2,1)} %get-tuple-element.26.dv_in) | copy-start | bytes 3145732
  66.5 0.8 copy-start.3

commit v3 on v2

--- a/solution.py
+++ b/solution.py
@@ -15,6 +15,7 @@
 WIDE = GROUP * HD
 KEEP = 2048
 SUB_LANES = 128
+DEEP = 4
 NEGATIVE = -1e30
 MESH = pl.DeviceIdType.MESH
 MIB = 1024 * 1024
@@ -52,7 +53,7 @@
     y_count, z_count, chunks,
     tokens, weight, routes, counts, query, key_in, value_in, attn_out, grad_out,
     q_all, do_all, de_all, k_all, v_all, c_all, part,
-    tok_v, cot_v, attn_v, dout_v, de_v, cnt_v, picked_v,
+    tok_v, cot_v, attn_v, dout_v, de_v, cnt_v, picked_v, q_own, k_own, v_own,
     tok_sem, in_sem, own_sem, y_send, y_recv, ring_send, ring_recv, c_send, c_recv,
 ):
     y, z = place(z_count)
@@ -67,6 +68,21 @@
     y_peers = [(y + step) % y_count for step in range(1, y_count)]
     greet([at(other, z) for other in y_peers] + [at(y, right), at(y, left)])
 
+    cnt_v[...] = jnp.full(cnt_v.shape, counts[0, 0], jnp.int32)
+
+    def wide(ref, g):
+        return ref.at[:, pl.ds(pl.multiple_of(g * WIDE, WIDE), WIDE)]
+
+    def narrow(ref, g):
+        return ref.at[:, pl.ds(pl.multiple_of(g * HD, HD), HD)]
+
+    own_in = [
+        pltpu.make_async_copy(narrow(key_in, y), k_own, own_sem.at[0]),
+        pltpu.make_async_copy(narrow(value_in, y), v_own, own_sem.at[1]),
+        pltpu.make_async_copy(wide(query, y), q_own, own_sem.at[2]),
+    ]
+    for copy in own_in:
+        copy.start()
     loads = []
     for c in range(chunks):
         loads.append(pltpu.make_async_copy(tokens.at[:, pl.ds(c * chunk, chunk)], tok_v.at[c], tok_sem.at[c]))
@@ -78,19 +94,13 @@
                 pltpu.make_async_copy(source.at[:, pl.ds(g * WIDE, WIDE)], target.at[g], in_sem.at[a, g])
             )
             rows_in[-1].start()
-    cnt_v[...] = jnp.full(cnt_v.shape, counts[0, 0], jnp.int32)
-
-    def wide(ref, g):
-        return ref.at[:, pl.ds(pl.multiple_of(g * WIDE, WIDE), WIDE)]
-
-    def narrow(ref, g):
-        return ref.at[:, pl.ds(pl.multiple_of(g * HD, HD), HD)]
-
+    for copy in own_in:
+        copy.wait()
     own = [
-        pltpu.make_async_copy(narrow(key_in, y), k_all.at[z, y], own_sem.at[0]),
-        pltpu.make_async_copy(narrow(value_in, y), v_all.at[z, y], own_sem.at[1]),
-        pltpu.make_async_copy(cnt_v, c_all.at[z, y], own_sem.at[2]),
-        pltpu.make_async_copy(wide(query, y), q_all.at[y], own_sem.at[3]),
+        pltpu.make_async_copy(k_own, k_all.at[z, y], own_sem.at[0]),
+        pltpu.make_async_copy(v_own, v_all.at[z, y], own_sem.at[1]),
+        pltpu.make_async_copy(cnt_v, c_all.at[z, y], own_sem.at[3]),
+        pltpu.make_async_copy(q_own, q_all.at[y], own_sem.at[2]),
     ]
     for copy in own:
         copy.start()
@@ -254,6 +264,9 @@
             pltpu.VMEM((y_count, GROUP, cap), f32),
             pltpu.VMEM((1, HD), jnp.int32),
             pltpu.VMEM((chunks, cap, width // chunks), f32),
+            pltpu.VMEM((cap, WIDE), bf16),
+            pltpu.VMEM((cap, HD), bf16),
+            pltpu.VMEM((cap, HD), bf16),
             pltpu.SemaphoreType.DMA((chunks,)),
             pltpu.SemaphoreType.DMA((2, y_count)),
             pltpu.SemaphoreType.DMA((6,)),
@@ -273,11 +286,18 @@
 
 def attention_kernel(
     y_count, z_count, block_rows, block_keys,
-    counts, q_in, do_in, de_in, k_in, v_in,
-    dq_out, dk_out, dv_out,
+    counts, q_hbm, do_hbm, de_hbm, k_hbm, v_hbm,
+    dq_hbm, dk_hbm, dv_hbm,
+    q_in, do_in, de_in, k_in, v_in, dq_out, dk_out, dv_out, in_sem, out_sem,
     row_f, do_f, de_f, q_b, do_b, de_b, k_f, v_f, k_b, kt_b, v_b, exps, tops, best, total, dk_f, dv_f, dq_f,
     s_even, s_odd, p_even, p_odd, ds_even, ds_odd, pair_row, pair_key, shard_start,
 ):
+    loads = []
+    for i, (source, target) in enumerate(
+        ((k_hbm, k_in), (v_hbm, v_in), (q_hbm, q_in), (do_hbm, do_in), (de_hbm, de_in))
+    ):
+        loads.append(pltpu.make_async_copy(source, target, in_sem.at[i]))
+        loads[-1].start()
     cap = q_in.shape[1]
     z = lax.axis_index("seq") % z_count
     shard_count = y_count * z_count
@@ -297,6 +317,9 @@
 
     lax.fori_loop(0, shard_count, add_counts, jnp.int32(0))
 
+    loads[0].wait()
+    loads[1].wait()
+
     def pack_keys(step, carry):
         for more in range(4):
             shard = step * 4 + more
@@ -333,6 +356,8 @@
             found = jnp.where(row >= row_start[yy], row + shift[yy], found)
         return found
 
+    for load in loads[2:]:
+        load.wait()
     for yy in range(y_count):
         rows = pl.ds(row_start[yy], cap)
         for h in range(GROUP):
@@ -416,17 +441,17 @@
             best[b, :, cols] = after
             total[b, :, cols] = total[b, :, cols] * jnp.exp2(before - after) + jnp.sum(grown, axis=0)
 
-    def two_scores(masked, j, carry):
-        n = 2 * j
-        raw(n + 1, 1)
-        grow(masked, n, 0)
-        raw(n + 2, 0)
-        grow(masked, n + 1, 1)
+    def some_scores(masked, many, j, carry):
+        for more in range(many):
+            n = many * j + more
+            raw(n + 1, (more + 1) % 2)
+            grow(masked, n, more % 2)
         return carry
 
     raw(0, 0)
-    lax.fori_loop(0, whole_pairs // 2, functools.partial(two_scores, False), 0)
-    lax.fori_loop(whole_pairs // 2, (pairs + 1) // 2, functools.partial(two_scores, True), 0)
+    whole_steps = whole_pairs // DEEP
+    lax.fori_loop(0, whole_steps, functools.partial(some_scores, False, DEEP), 0)
+    lax.fori_loop(whole_steps * (DEEP // 2), (pairs + 1) // 2, functools.partial(some_scores, True, 2), 0)
 
     def finish_rows(b, carry):
         top = jnp.max(best[b], axis=0, keepdims=True)
@@ -451,39 +476,26 @@
         dk_f[kb] += jnp.dot(score_grad, q_b[b], preferred_element_type=f32)
         dq_f[b] += jnp.dot(kt_b[kb], score_grad, preferred_element_type=f32)
 
-    def two_pairs(j, carry):
-        n = 2 * j
-        products(n, 0)
-        terms(n + 1, 1)
-        products(n + 1, 1)
-        terms(n + 2, 0)
+    def some_pairs(many, j, carry):
+        for more in range(many):
+            n = many * j + more
+            products(n, more % 2)
+            terms(n + 1, (more + 1) % 2)
         return carry
 
     @pl.when(pairs > 0)
     def _():
         terms(0, 0)
 
-    lax.fori_loop(0, pairs // 2, two_pairs, 0)
+    steps = pairs // DEEP
+    lax.fori_loop(0, steps, functools.partial(some_pairs, DEEP), 0)
+    lax.fori_loop(steps * (DEEP // 2), pairs // 2, functools.partial(some_pairs, 2), 0)
 
     @pl.when(pairs % 2 == 1)
     def _():
         products(pairs - 1, 0)
 
-    def turn_rows(b, carry):
-        rows = pl.ds(pl.multiple_of(b * block_rows, block_rows), block_rows)
-        turned = dq_f[b].T * root
-        for h in range(GROUP):
-            row_f[h, rows, :] = turned[h * block_rows : (h + 1) * block_rows, :]
-        return carry
-
-    lax.fori_loop(0, row_blocks, turn_rows, 0)
-
     slot = lax.broadcasted_iota(jnp.int32, (cap, 1), 0)
-    for yy in range(y_count):
-        rows = pl.ds(row_start[yy], cap)
-        for h in range(GROUP):
-            grad = jnp.where(slot < live[yy], row_f[h, rows, :], 0.0)
-            dq_out[yy, :, h * HD : (h + 1) * HD] = grad.astype(bf16)
 
     def widen_keys(b, carry):
         rows = pl.ds(pl.multiple_of(b * block_keys, block_keys), block_keys)
@@ -504,6 +516,32 @@
         return carry
 
     lax.fori_loop(0, shard_count // 4, unpack_keys, 0)
+    stores = [
+        pltpu.make_async_copy(dk_out, dk_hbm, out_sem.at[0]),
+        pltpu.make_async_copy(dv_out, dv_hbm, out_sem.at[1]),
+        pltpu.make_async_copy(dq_out, dq_hbm, out_sem.at[2]),
+    ]
+    stores[0].start()
+    stores[1].start()
+
+    def turn_rows(b, carry):
+        rows = pl.ds(pl.multiple_of(b * block_rows, block_rows), block_rows)
+        turned = dq_f[b].T * root
+        for h in range(GROUP):
+            row_f[h, rows, :] = turned[h * block_rows : (h + 1) * block_rows, :]
+        return carry
+
+    lax.fori_loop(0, row_blocks, turn_rows, 0)
+
+    for yy in range(y_count):
+        rows = pl.ds(row_start[yy], cap)
+        for h in range(GROUP):
+            grad = jnp.where(slot < live[yy], row_f[h, rows, :], 0.0)
+            dq_out[yy, :, h * HD : (h + 1) * HD] = grad.astype(bf16)
+
+    stores[2].start()
+    for store in stores:
+        store.wait()
 
 
 def attention(y_count, z_count, counts, q_in, do_in, de_in, k_in, v_in):
@@ -513,7 +551,7 @@
     most = y_count * cap
     row_blocks = most // block_rows
     key_blocks = KEEP // block_keys
-    vmem = pl.BlockSpec(memory_space=pltpu.VMEM)
+    anywhere = pl.BlockSpec(memory_space=pl.ANY)
     bf16, f32 = jnp.bfloat16, jnp.float32
     shape = jax.ShapeDtypeStruct
     return pl.pallas_call(
@@ -523,9 +561,19 @@
             shape((z_count, y_count, cap, HD), bf16),
             shape((z_count, y_count, cap, HD), bf16),
         ),
-        in_specs=[pl.BlockSpec(memory_space=pltpu.SMEM)] + [vmem] * 5,
-        out_specs=(vmem,) * 3,
+        in_specs=[pl.BlockSpec(memory_space=pltpu.SMEM)] + [anywhere] * 5,
+        out_specs=(anywhere,) * 3,
         scratch_shapes=[
+            pltpu.VMEM((y_count, cap, WIDE), bf16),
+            pltpu.VMEM((y_count, cap, WIDE), bf16),
+            pltpu.VMEM((y_count, GROUP, cap), f32),
+            pltpu.VMEM((z_count, y_count, cap, HD), bf16),
+            pltpu.VMEM((z_count, y_count, cap, HD), bf16),
+            pltpu.VMEM((y_count, cap, WIDE), bf16),
+            pltpu.VMEM((z_count, y_count, cap, HD), bf16),
+            pltpu.VMEM((z_count, y_count, cap, HD), bf16),
+            pltpu.SemaphoreType.DMA((5,)),
+            pltpu.SemaphoreType.DMA((3,)),
             pltpu.VMEM((GROUP, most + cap, HD), f32),
             pltpu.VMEM((GROUP, most + cap, HD), f32),
             pltpu.VMEM((most + cap, HD), f32),
@@ -561,9 +609,9 @@
 
 def scatter_kernel(
     y_count, z_count, dp_count,
-    dq_in, dk_in, dv_in, part,
-    dq_out, dk_out, dv_out, router_out,
-    held, fin, dp_held, y_held, z_held, dp_sum, y_sum,
+    dq_in, dk_hbm, dv_hbm, part,
+    dq_out, dk_out, dv_out, router_out, dk_in, dv_in,
+    held, fin, dp_held, y_held, z_held, dp_sum, y_sum, dq_own,
     own_sem, q_send, q_recv, ring_send, ring_recv, fin_send, fin_recv, r_send, r_recv,
 ):
     y, z = place(z_count)
@@ -587,7 +635,16 @@
     def narrow(ref, g):
         return ref.at[:, pl.ds(pl.multiple_of(g * HD, HD), HD)]
 
-    own = [pltpu.make_async_copy(dq_in.at[y], wide(dq_out, y), own_sem.at[0])]
+    own_in = [
+        pltpu.make_async_copy(dk_hbm, dk_in, own_sem.at[1]),
+        pltpu.make_async_copy(dv_hbm, dv_in, own_sem.at[2]),
+        pltpu.make_async_copy(dq_in.at[y], dq_own, own_sem.at[0]),
+    ]
+    for copy in own_in:
+        copy.start()
+    for copy in own_in:
+        copy.wait()
+    own = [pltpu.make_async_copy(dq_own, wide(dq_out, y), own_sem.at[0])]
     own[0].start()
     pl.semaphore_wait(pltpu.get_barrier_semaphore(), len(peers))
 
@@ -698,9 +755,11 @@
             shape((cap, KV * HD), bf16),
             shape(small, f32),
         ),
-        in_specs=[anywhere, vmem, vmem, vmem],
+        in_specs=[anywhere, anywhere, anywhere, vmem],
         out_specs=(anywhere, anywhere, anywhere, vmem),
         scratch_shapes=[
+            pltpu.VMEM((z_count, y_count, cap, HD), bf16),
+            pltpu.VMEM((z_count, y_count, cap, HD), bf16),
             pltpu.VMEM((4, longer, y_count, cap, HD), bf16),
             pltpu.VMEM((2, y_count, cap, HD), bf16),
             pltpu.VMEM((dp_count,) + small, f32),
@@ -708,6 +767,7 @@
             pltpu.VMEM((z_count,) + small, f32),
             pltpu.VMEM(small, f32),
             pltpu.VMEM(small, f32),
+            pltpu.VMEM((cap, WIDE), bf16),
             pltpu.SemaphoreType.DMA((3,)),
             pltpu.SemaphoreType.DMA((y_count - 1,)),
             pltpu.SemaphoreType.DMA((y_count - 1,)),
@@ -719,10 +779,49 @@
             pltpu.SemaphoreType.DMA((router_copies,)),
         ],
         compiler_params=pltpu.CompilerParams(
-            collective_id=1, has_side_effects=True, vmem_limit_bytes=32 * MIB
+            collective_id=1, has_side_effects=True, vmem_limit_bytes=63 * MIB
         ),
         name="scatter",
     )(dq_in, dk_in, dv_in, part)
+
+
+def result_kernel(dq_in, dk_in, dv_in, dq_out, dk_out, dv_out, dq_v, dk_v, dv_v, in_sem, out_sem):
+    moves = []
+    rows = dq_v.shape[1]
+    for i in range(dq_v.shape[0]):
+        part = pl.ds(i * rows, rows)
+        moves.append((dq_in.at[part], dq_v.at[i], dq_out.at[part]))
+    moves += [(dk_in, dk_v, dk_out), (dv_in, dv_v, dv_out)]
+    loads = [pltpu.make_async_copy(a, b, in_sem.at[i]) for i, (a, b, _) in enumerate(moves)]
+    stores = [pltpu.make_async_copy(b, c, out_sem.at[i]) for i, (_, b, c) in enumerate(moves)]
+    for load in loads:
+        load.start()
+    for load, store in zip(loads, stores):
+        load.wait()
+        store.start()
+    for store in stores:
+        store.wait()
+
+
+def results(dq, dk, dv):
+    anywhere = pl.BlockSpec(memory_space=pl.ANY)
+    pieces = 4
+    shape = jax.ShapeDtypeStruct
+    return pl.pallas_call(
+        result_kernel,
+        out_shape=tuple(shape(x.shape, x.dtype) for x in (dq, dk, dv)),
+        in_specs=[anywhere] * 3,
+        out_specs=(anywhere,) * 3,
+        scratch_shapes=[
+            pltpu.VMEM((pieces, dq.shape[0] // pieces, dq.shape[1]), dq.dtype),
+            pltpu.VMEM(dk.shape, dk.dtype),
+            pltpu.VMEM(dv.shape, dv.dtype),
+            pltpu.SemaphoreType.DMA((pieces + 2,)),
+            pltpu.SemaphoreType.DMA((pieces + 2,)),
+        ],
+        compiler_params=pltpu.CompilerParams(vmem_limit_bytes=63 * MIB),
+        name="results",
+    )(dq, dk, dv)
 
 
 def on_device(tokens, router_weight, routes, counts, query, key_in, value_in, attn_out, grad_out):
@@ -736,6 +835,7 @@
     )
     dq, dk, dv = attention(y_count, z_count, c_all, q_all, do_all, de_all, k_all, v_all)
     dq, dk, dv, router = scatter(y_count, z_count, dp_count, dq, dk, dv, part)
+    dq, dk, dv = results(dq, dk, dv)
     share = width // (dp_count * y_count * z_count)
     router = lax.dynamic_slice(router.reshape(-1), (lax.axis_index("seq") * share,), (share,))
     return (dq[None], dk[None], dv[None], router)

time: 111 us -> 105 us (0.946); the launches traced: 109 us -> 104 us
  local copies, waits for them, and re-layouts: 7.3 us -> 1.26 us
  Pallas kernels: 100 us -> 102 us
    unnamed x11 -> x0, local copies, waits for them, and re-layouts: 6.71 us -> none
    pallas_call x1, Pallas kernels: 38.6 us -> 35.2 us  [scatter(): pl.pallas_call(functools.partial(scatter_kernel, y_count, z_count, dp_cou...]
    pallas_call x0 -> x1, Pallas kernels: none -> 2.1 us  [results(): pl.pallas_call(result_kernel, out_shape=tuple((shape(x.shape, x.dtype) fo...]
    pallas_call x1, Pallas kernels: 37.7 us -> 39.8 us  [gather(): pl.pallas_call(functools.partial(gather_kernel, y_count, z_count, chunks)...]
where the time goes in v3:
time: 105 us; the launch traced here: 104 us
  Pallas kernels  102 us (97%)
  between operations  1.31 us (1%)
  local copies, waits for them, and re-layouts  1.26 us (1%)
    pallas_call x1, Pallas kernels, gather(): pl.pallas_call(functools.partial(gather_kernel, y_count, z_count, chunks)...  39.8 us
    pallas_call x1, Pallas kernels, scatter(): pl.pallas_call(functools.partial(scatter_kernel, y_count, z_count, dp_cou...  35.2 us
    pallas_call x1, Pallas kernels, attention(): pl.pallas_call(functools.partial(attention_kernel, y_count, z_count, bloc...  24.5 us

profile of v3, /device:TPU:6, one launch (start us, length us, event | category | flops | bytes accessed | tf_op | source)
XLA Modules:
  0.0 104.1 jit_solution(2306553774449227545)
XLA Ops:
  1.3 39.8 %gather.1 = (bf16[4,128,1024]{2,1,0:T(8,128)(2,1)}, bf16[4,128,1024]{2,1,0:T(8,128)(2,1)}, f32[4,8,128]{2,1,0:T(8,128)}, bf16[8,4,128,128]{3,2,1,0:T(8,128)(2,1)...) custom-call(bf16[512,5120]{1,0:T(8,128)(2,1)} %bitcast.11, ...), custom_call_target="tpu_custom_call" | custom-call | tf_op jit(solution)/shard_map/gather/pallas_call | solution.py:246
  41.1 24.5 %attention.1 = (bf16[4,128,1024]{2,1,0:T(8,128)(2,1)}, bf16[8,4,128,128]{3,2,1,0:T(8,128)(2,1)}, bf16[8,4,128,128]{3,2,1,0:T(8,128)(2,1)}) custom-call(s32[8,4,1,128]{3,2,1,0:T(1,128)} %get-tuple-element.21.counts, bf16[4,128,1024]{2,1,0:T(8,128)(2,1)} %get-tuple-element.22.q_hbm, bf16[4,128,1024]{2,1,0:T(8,128)(2,1)} %get-tuple-element.23.do_hbm, ...), custom_call_target="tpu_custom_call" | custom-call | tf_op jit(solution)/shard_map/attention/pallas_call | solution.py:557
  65.6 35.2 %scatter.1 = (bf16[128,4096]{1,0:T(8,128)(2,1)}, bf16[128,512]{1,0:T(8,128)(2,1)}, bf16[128,512]{1,0:T(8,128)(2,1)}, f32[5,128]{1,0:T(8,128)}) custom-call(bf16[4,128,1024]{2,1,0:T(8,128)(2,1)} %get-tuple-element.27.dq_in, bf16[8,4,128,128]{3,2,1,0:T(8,128)(2,1)} %get-tuple-element.28.dk_hbm, bf16[8,4,128,128]{3,2,1,0:T(8,128)(2,1)} %get-tuple-element.29.dv_hbm, ...), custom_call_target="tpu_custom_call" | custom-call | tf_op jit(solution)/shard_map/scatter/pallas_call | solution.py:750
  100.8 2.1 %results.1 = (bf16[128,4096]{1,0:T(8,128)(2,1)}, bf16[128,512]{1,0:T(8,128)(2,1)}, bf16[128,512]{1,0:T(8,128)(2,1)}) custom-call(bf16[128,4096]{1,0:T(8,128)(2,1)} %get-tuple-element.31.dq_in, bf16[128,512]{1,0:T(8,128)(2,1)} %get-tuple-element.32.dk_in, bf16[128,512]{1,0:T(8,128)(2,1)} %get-tuple-element.33.dv_in), custom_call_target="tpu_custom_call" | custom-call | tf_op jit(solution)/shard_map/results/pallas_call | solution.py:810
  102.9 1.3 %dynamic_slice.3 = f32[20]{0:T(128)} dynamic-slice(f32[640]{0:T(1024)} %bitcast.21, s32[]{:T(128)S(6)} %select_n.3), dynamic_slice_sizes={20} | dynamic-slice | bytes 164 | tf_op jit(solution)/shard_map/dynamic_slice | solution.py:840

commit v4 on v3

--- a/solution.py
+++ b/solution.py
@@ -15,7 +15,7 @@
 WIDE = GROUP * HD
 KEEP = 2048
 SUB_LANES = 128
-DEEP = 4
+DEEP = (8, 4, 2)
 NEGATIVE = -1e30
 MESH = pl.DeviceIdType.MESH
 MIB = 1024 * 1024
@@ -94,16 +94,6 @@
                 pltpu.make_async_copy(source.at[:, pl.ds(g * WIDE, WIDE)], target.at[g], in_sem.at[a, g])
             )
             rows_in[-1].start()
-    for copy in own_in:
-        copy.wait()
-    own = [
-        pltpu.make_async_copy(k_own, k_all.at[z, y], own_sem.at[0]),
-        pltpu.make_async_copy(v_own, v_all.at[z, y], own_sem.at[1]),
-        pltpu.make_async_copy(cnt_v, c_all.at[z, y], own_sem.at[3]),
-        pltpu.make_async_copy(q_own, q_all.at[y], own_sem.at[2]),
-    ]
-    for copy in own:
-        copy.start()
     pl.semaphore_wait(pltpu.get_barrier_semaphore(), y_count + 1)
 
     first = []
@@ -122,6 +112,16 @@
     for i, other in enumerate(y_peers):
         late.append(remote(wide(query, other), q_all.at[y], y_send.at[3, i], y_recv.at[3, i], at(other, z)))
         late[-1].start()
+    own = [
+        pltpu.make_async_copy(k_own, k_all.at[z, y], own_sem.at[0]),
+        pltpu.make_async_copy(v_own, v_all.at[z, y], own_sem.at[1]),
+        pltpu.make_async_copy(cnt_v, c_all.at[z, y], own_sem.at[3]),
+        pltpu.make_async_copy(q_own, q_all.at[y], own_sem.at[2]),
+    ]
+    for copy in own_in:
+        copy.wait()
+    for copy in own:
+        copy.start()
     for copy in own[:3]:
         copy.wait()
     for copy in first:
@@ -311,11 +311,10 @@
     def count_of(shard):
         return counts[shard % z_count, shard // z_count, 0, 0]
 
-    def add_counts(shard, offset):
-        shard_start[shard] = offset
-        return offset + count_of(shard)
-
-    lax.fori_loop(0, shard_count, add_counts, jnp.int32(0))
+    keys_before = jnp.int32(0)
+    for shard in range(shard_count):
+        shard_start[shard] = keys_before
+        keys_before = keys_before + count_of(shard)
 
     loads[0].wait()
     loads[1].wait()
@@ -449,9 +448,11 @@
         return carry
 
     raw(0, 0)
-    whole_steps = whole_pairs // DEEP
-    lax.fori_loop(0, whole_steps, functools.partial(some_scores, False, DEEP), 0)
-    lax.fori_loop(whole_steps * (DEEP // 2), (pairs + 1) // 2, functools.partial(some_scores, True, 2), 0)
+    done = jnp.int32(0)
+    for many in DEEP:
+        lax.fori_loop(done // many, whole_pairs // many, functools.partial(some_scores, False, many), 0)
+        done = whole_pairs // many * many
+    lax.fori_loop(done // 2, (pairs + 1) // 2, functools.partial(some_scores, True, 2), 0)
 
     def finish_rows(b, carry):
         top = jnp.max(best[b], axis=0, keepdims=True)
@@ -487,9 +488,10 @@
     def _():
         terms(0, 0)
 
-    steps = pairs // DEEP
-    lax.fori_loop(0, steps, functools.partial(some_pairs, DEEP), 0)
-    lax.fori_loop(steps * (DEEP // 2), pairs // 2, functools.partial(some_pairs, 2), 0)
+    done = jnp.int32(0)
+    for many in DEEP:
+        lax.fori_loop(done // many, pairs // many, functools.partial(some_pairs, many), 0)
+        done = pairs // many * many
 
     @pl.when(pairs % 2 == 1)
     def _():
@@ -642,20 +644,17 @@
     ]
     for copy in own_in:
         copy.start()
-    for copy in own_in:
-        copy.wait()
-    own = [pltpu.make_async_copy(dq_own, wide(dq_out, y), own_sem.at[0])]
-    own[0].start()
     pl.semaphore_wait(pltpu.get_barrier_semaphore(), len(peers))
 
     plan = ring_plan(z_count)
     mine = (dk_in, dv_in)
+    apart = (dk_hbm, dv_hbm)
 
     def ring_copy(lane, step):
         array, way, steps = plan[lane]
         block = (z + way * (steps - step) + z_count) % z_count
         there = at(y, right if way == 1 else left)
-        source = mine[array].at[block] if step == 0 else held.at[lane, step - 1]
+        source = apart[array].at[block] if step == 0 else held.at[lane, step - 1]
         return remote(source, held.at[lane, step], ring_send.at[lane, step], ring_recv.at[lane, step], there)
 
     def forward(step):
@@ -674,6 +673,10 @@
     for i, other in enumerate(y_peers):
         sends.append(remote(dq_in.at[other], wide(dq_out, y), q_send.at[i], q_recv.at[i], at(other, z)))
         sends[-1].start()
+    for copy in own_in:
+        copy.wait()
+    own = [pltpu.make_async_copy(dq_own, wide(dq_out, y), own_sem.at[0])]
+    own[0].start()
 
     def share(first, source_of, held_ref, peers_there, me):
         copies = []
@@ -785,7 +788,9 @@
     )(dq_in, dk_in, dv_in, part)
 
 
-def result_kernel(dq_in, dk_in, dv_in, dq_out, dk_out, dv_out, dq_v, dk_v, dv_v, in_sem, out_sem):
+def result_kernel(
+    dq_in, dk_in, dv_in, router, dq_out, dk_out, dv_out, share, dq_v, dk_v, dv_v, in_sem, out_sem
+):
     moves = []
     rows = dq_v.shape[1]
     for i in range(dq_v.shape[0]):
@@ -796,6 +801,13 @@
     stores = [pltpu.make_async_copy(b, c, out_sem.at[i]) for i, (_, b, c) in enumerate(moves)]
     for load in loads:
         load.start()
+    first = lax.axis_index("seq") * share.shape[1]
+    lane = lax.broadcasted_iota(jnp.int32, (1, HD), 1)
+    here = jnp.zeros((1, HD), jnp.float32)
+    for row in range(router.shape[0]):
+        turned = pltpu.roll(router[row : row + 1, :], (HD - first % HD) % HD, 1)
+        here = jnp.where((first + lane) // HD == row, turned, here)
+    share[...] = here[:, : share.shape[1]]
     for load, store in zip(loads, stores):
         load.wait()
         store.start()
@@ -803,15 +815,16 @@
         store.wait()
 
 
-def results(dq, dk, dv):
+def results(share, dq, dk, dv, router):
+    vmem = pl.BlockSpec(memory_space=pltpu.VMEM)
     anywhere = pl.BlockSpec(memory_space=pl.ANY)
     pieces = 4
     shape = jax.ShapeDtypeStruct
     return pl.pallas_call(
         result_kernel,
-        out_shape=tuple(shape(x.shape, x.dtype) for x in (dq, dk, dv)),
-        in_specs=[anywhere] * 3,
-        out_specs=(anywhere,) * 3,
+        out_shape=tuple(shape(x.shape, x.dtype) for x in (dq, dk, dv)) + (shape((1, share), jnp.float32),),
+        in_specs=[anywhere] * 3 + [vmem],
+        out_specs=(anywhere,) * 3 + (vmem,),
         scratch_shapes=[
             pltpu.VMEM((pieces, dq.shape[0] // pieces, dq.shape[1]), dq.dtype),
             pltpu.VMEM(dk.shape, dk.dtype),
@@ -821,7 +834,7 @@
         ],
         compiler_params=pltpu.CompilerParams(vmem_limit_bytes=63 * MIB),
         name="results",
-    )(dq, dk, dv)
+    )(dq, dk, dv, router)
 
 
 def on_device(tokens, router_weight, routes, counts, query, key_in, value_in, attn_out, grad_out):
@@ -835,10 +848,9 @@
     )
     dq, dk, dv = attention(y_count, z_count, c_all, q_all, do_all, de_all, k_all, v_all)
     dq, dk, dv, router = scatter(y_count, z_count, dp_count, dq, dk, dv, part)
-    dq, dk, dv = results(dq, dk, dv)
     share = width // (dp_count * y_count * z_count)
-    router = lax.dynamic_slice(router.reshape(-1), (lax.axis_index("seq") * share,), (share,))
-    return (dq[None], dk[None], dv[None], router)
+    dq, dk, dv, router = results(share, dq, dk, dv, router)
+    return (dq[None], dk[None], dv[None], router[0])
 
 
 def solution(mesh):

time: 105 us -> 102 us (0.971)
  Pallas kernels: 102 us -> 100 us
  local copies, waits for them, and re-layouts: 1.26 us -> 0 us
    pallas_call x1, Pallas kernels: 24.5 us -> 16 us  [attention(): pl.pallas_call(functools.partial(attention_kernel, y_count, z_count, bloc...]
    pallas_call x1, Pallas kernels: 35.2 us -> 43.1 us  [scatter(): pl.pallas_call(functools.partial(scatter_kernel, y_count, z_count, dp_cou...]
    pallas_call x1, Pallas kernels: 39.8 us -> 37.7 us  [gather(): pl.pallas_call(functools.partial(gather_kernel, y_count, z_count, chunks)...]
    dynamic_slice x1 -> x0, local copies, waits for them, and re-layouts: 1.26 us -> none  [on_device(): lax.dynamic_slice(router.reshape(-1), (lax.axis_index('seq') * share,), (...]
    pallas_call x1, Pallas kernels: 2.1 us -> 3.29 us  [results(): pl.pallas_call(result_kernel, out_shape=tuple((shape(x.shape, x.dtype) fo...]
where the time goes in v4:
time: 102 us; the launch traced here: 101 us
  Pallas kernels  100 us (98%)
  between operations  1.3 us (1%)
    pallas_call x1, Pallas kernels, scatter(): pl.pallas_call(functools.partial(scatter_kernel, y_count, z_count, dp_cou...  43.1 us
    pallas_call x1, Pallas kernels, gather(): pl.pallas_call(functools.partial(gather_kernel, y_count, z_count, chunks)...  37.7 us
    pallas_call x1, Pallas kernels, attention(): pl.pallas_call(functools.partial(attention_kernel, y_count, z_count, bloc...  16 us
    pallas_call x1, Pallas kernels, results(): pl.pallas_call(result_kernel, out_shape=tuple((shape(x.shape, x.dtype) fo...  3.29 us

profile of v4, /device:TPU:6, one launch (start us, length us, event | category | flops | bytes accessed | tf_op | source)
XLA Modules:
  0.0 101.4 jit_solution(10075272995790010141)
XLA Ops:
  1.3 37.7 %gather.1 = (bf16[4,128,1024]{2,1,0:T(8,128)(2,1)}, bf16[4,128,1024]{2,1,0:T(8,128)(2,1)}, f32[4,8,128]{2,1,0:T(8,128)}, bf16[8,4,128,128]{3,2,1,0:T(8,128)(2,1)...) custom-call(bf16[512,5120]{1,0:T(8,128)(2,1)} %bitcast.11, ...), custom_call_target="tpu_custom_call" | custom-call | tf_op jit(solution)/shard_map/gather/pallas_call | solution.py:246
  39.0 16.0 %attention.1 = (bf16[4,128,1024]{2,1,0:T(8,128)(2,1)}, bf16[8,4,128,128]{3,2,1,0:T(8,128)(2,1)}, bf16[8,4,128,128]{3,2,1,0:T(8,128)(2,1)}) custom-call(s32[8,4,1,128]{3,2,1,0:T(1,128)} %get-tuple-element.22.counts, bf16[4,128,1024]{2,1,0:T(8,128)(2,1)} %get-tuple-element.23.q_hbm, bf16[4,128,1024]{2,1,0:T(8,128)(2,1)} %get-tuple-element.24.do_hbm, ...), custom_call_target="tpu_custom_call" | custom-call | tf_op jit(solution)/shard_map/attention/pallas_call | solution.py:559
  55.0 43.1 %scatter.1 = (bf16[128,4096]{1,0:T(8,128)(2,1)}, bf16[128,512]{1,0:T(8,128)(2,1)}, bf16[128,512]{1,0:T(8,128)(2,1)}, f32[5,128]{1,0:T(8,128)}) custom-call(bf16[4,128,1024]{2,1,0:T(8,128)(2,1)} %get-tuple-element.28.dq_in, bf16[8,4,128,128]{3,2,1,0:T(8,128)(2,1)} %get-tuple-element.29.dk_hbm, bf16[8,4,128,128]{3,2,1,0:T(8,128)(2,1)} %get-tuple-element.30.dv_hbm, ...), custom_call_target="tpu_custom_call" | custom-call | tf_op jit(solution)/shard_map/scatter/pallas_call | solution.py:753
  98.1 3.3 %results.1 = (bf16[128,4096]{1,0:T(8,128)(2,1)}, bf16[128,512]{1,0:T(8,128)(2,1)}, bf16[128,512]{1,0:T(8,128)(2,1)}, f32[1,20]{1,0:T(1,128)}) custom-call(bf16[128,4096]{1,0:T(8,128)(2,1)} %get-tuple-element.32.dq_in, bf16[128,512]{1,0:T(8,128)(2,1)} %get-tuple-element.33.dk_in, bf16[128,512]{1,0:T(8,128)(2,1)} %get-tuple-element.34.dv_in, ...), custom_call_target="tpu_custom_call" | custom-call | tf_op jit(solution)/shard_map/results/pallas_call | solution.py:823

commit v5 on v4

--- a/solution.py
+++ b/solution.py
@@ -288,8 +288,8 @@
     y_count, z_count, block_rows, block_keys,
     counts, q_hbm, do_hbm, de_hbm, k_hbm, v_hbm,
     dq_hbm, dk_hbm, dv_hbm,
-    q_in, do_in, de_in, k_in, v_in, dq_out, dk_out, dv_out, in_sem, out_sem,
-    row_f, do_f, de_f, q_b, do_b, de_b, k_f, v_f, k_b, kt_b, v_b, exps, tops, best, total, dk_f, dv_f, dq_f,
+    q_in, do_in, de_in, k_in, v_in, dk_out, dv_out, in_sem, out_sem,
+    q_b, do_b, de_b, k_f, v_f, k_b, kt_b, v_b, exps, tops, best, total, dk_f, dv_f, dq_f,
     s_even, s_odd, p_even, p_odd, ds_even, ds_odd, pair_row, pair_key, shard_start,
 ):
     loads = []
@@ -316,19 +316,17 @@
         shard_start[shard] = keys_before
         keys_before = keys_before + count_of(shard)
 
-    loads[0].wait()
-    loads[1].wait()
-
-    def pack_keys(step, carry):
+    def pack(source, target, step, carry):
         for more in range(4):
             shard = step * 4 + more
-            zz, yy = shard % z_count, shard // z_count
             rows = pl.ds(shard_start[shard], cap)
-            k_f[rows, :] = k_in[zz, yy].astype(f32)
-            v_f[rows, :] = v_in[zz, yy].astype(f32)
+            target[rows, :] = source[shard % z_count, shard // z_count].astype(f32)
         return carry
 
-    lax.fori_loop(0, shard_count // 4, pack_keys, 0)
+    loads[0].wait()
+    lax.fori_loop(0, shard_count // 4, functools.partial(pack, k_in, k_f), 0)
+    loads[1].wait()
+    lax.fori_loop(0, shard_count // 4, functools.partial(pack, v_in, v_f), 0)
 
     def narrow_keys(b, carry):
         rows = pl.ds(b * block_keys, block_keys)
@@ -341,56 +339,33 @@
 
     lax.fori_loop(0, key_blocks, narrow_keys, 0)
 
-    row_start, shift, live = [], [], []
-    rows_here = 0
-    for yy in range(y_count):
-        row_start.append(rows_here)
-        shift.append(shard_start[yy * z_count + z] - rows_here)
-        live.append(counts[z, yy, 0, 0])
-        rows_here = rows_here + live[yy]
-
-    def place_of(row):
-        found = row + shift[0]
-        for yy in range(1, y_count):
-            found = jnp.where(row >= row_start[yy], row + shift[yy], found)
-        return found
+    halves = cap // block_rows
+    row_blocks = y_count * halves
+
+    def first_place(b):
+        return shard_start[b // halves * z_count + z] + b % halves * block_rows
+
+    def live_rows(b):
+        return jnp.clip(counts[z, b // halves, 0, 0] - b % halves * block_rows, 0, block_rows)
 
     for load in loads[2:]:
         load.wait()
-    for yy in range(y_count):
-        rows = pl.ds(row_start[yy], cap)
+    for b in range(row_blocks):
+        here = slice(b % halves * block_rows, (b % halves + 1) * block_rows)
         for h in range(GROUP):
-            cols = slice(h * HD, (h + 1) * HD)
-            row_f[h, rows, :] = q_in[yy, :, cols].astype(f32)
-            do_f[h, rows, :] = do_in[yy, :, cols].astype(f32)
-        padded = jnp.concatenate([de_in[yy], jnp.zeros((HD - GROUP, cap), f32)], axis=0)
-        de_f[rows, :] = padded.T
-    tail = pl.ds(rows_here, block_rows)
-    for h in range(GROUP):
-        row_f[h, tail, :] = jnp.zeros((block_rows, HD), f32)
-        do_f[h, tail, :] = jnp.zeros((block_rows, HD), f32)
-    de_f[tail, :] = jnp.zeros((block_rows, HD), f32)
-
-    row_blocks = (rows_here + block_rows - 1) // block_rows
-
-    def narrow_rows(b, carry):
-        rows = pl.ds(pl.multiple_of(b * block_rows, block_rows), block_rows)
-        across = de_f[rows, :].T
-        for h in range(GROUP):
-            mine = slice(h * block_rows, (h + 1) * block_rows)
-            q_b[b, mine, :] = row_f[h, rows, :].astype(bf16)
-            do_b[b, mine, :] = do_f[h, rows, :].astype(bf16)
-            de_b[b, :, mine] = across[h : h + 1, :]
-        return carry
-
-    lax.fori_loop(0, row_blocks, narrow_rows, 0)
+            mine, cols = slice(h * block_rows, (h + 1) * block_rows), slice(h * HD, (h + 1) * HD)
+            q_b[b, mine, :] = q_in[b // halves, here, cols]
+            do_b[b, mine, :] = do_in[b // halves, here, cols]
+            de_b[b, :, mine] = de_in[b // halves, h : h + 1, here]
 
     nt = (((1,), (1,)), ((), ()))
 
     def list_pairs(masked, count):
         def of_rows(b, count):
-            full = (place_of(b * block_rows) + 1) // block_keys
-            used = place_of(jnp.minimum((b + 1) * block_rows, rows_here) - 1) // block_keys + 1
+            full = (first_place(b) + 1) // block_keys
+            used = (first_place(b) + live_rows(b) - 1) // block_keys + 1
+            used = jnp.where(live_rows(b) > 0, used, 0)
+            full = jnp.minimum(full, used)
 
             def add(kb, count):
                 pair_row[count] = b
@@ -428,7 +403,7 @@
             block = s_b[slot][:, cols] * power
             if masked:
                 lane = lax.broadcasted_iota(jnp.int32, (1, SUB_LANES), 1)
-                row_place = place_of(b * block_rows + lane % block_rows) - kb * block_keys
+                row_place = first_place(b) + lane % block_rows - kb * block_keys
                 key_place = lax.broadcasted_iota(jnp.int32, (block_keys, SUB_LANES), 0)
                 block = jnp.where(key_place <= row_place, block, NEGATIVE)
             block = block.reshape(block_keys // 8, 8, SUB_LANES)
@@ -497,6 +472,12 @@
     def _():
         products(pairs - 1, 0)
 
+    stores = [
+        pltpu.make_async_copy(dq_f, dq_hbm, out_sem.at[0]),
+        pltpu.make_async_copy(dk_out, dk_hbm, out_sem.at[1]),
+        pltpu.make_async_copy(dv_out, dv_hbm, out_sem.at[2]),
+    ]
+    stores[0].start()
     slot = lax.broadcasted_iota(jnp.int32, (cap, 1), 0)
 
     def widen_keys(b, carry):
@@ -518,30 +499,8 @@
         return carry
 
     lax.fori_loop(0, shard_count // 4, unpack_keys, 0)
-    stores = [
-        pltpu.make_async_copy(dk_out, dk_hbm, out_sem.at[0]),
-        pltpu.make_async_copy(dv_out, dv_hbm, out_sem.at[1]),
-        pltpu.make_async_copy(dq_out, dq_hbm, out_sem.at[2]),
-    ]
-    stores[0].start()
-    stores[1].start()
-
-    def turn_rows(b, carry):
-        rows = pl.ds(pl.multiple_of(b * block_rows, block_rows), block_rows)
-        turned = dq_f[b].T * root
-        for h in range(GROUP):
-            row_f[h, rows, :] = turned[h * block_rows : (h + 1) * block_rows, :]
-        return carry
-
-    lax.fori_loop(0, row_blocks, turn_rows, 0)
-
-    for yy in range(y_count):
-        rows = pl.ds(row_start[yy], cap)
-        for h in range(GROUP):
-            grad = jnp.where(slot < live[yy], row_f[h, rows, :], 0.0)
-            dq_out[yy, :, h * HD : (h + 1) * HD] = grad.astype(bf16)
-
-    stores[2].start()
+    for store in stores[1:]:
+        store.start()
     for store in stores:
         store.wait()
 
@@ -559,7 +518,7 @@
     return pl.pallas_call(
         functools.partial(attention_kernel, y_count, z_count, block_rows, block_keys),
         out_shape=(
-            shape((y_count, cap, WIDE), bf16),
+            shape((row_blocks, HD, lanes), f32),
             shape((z_count, y_count, cap, HD), bf16),
             shape((z_count, y_count, cap, HD), bf16),
         ),
@@ -571,14 +530,10 @@
             pltpu.VMEM((y_count, GROUP, cap), f32),
             pltpu.VMEM((z_count, y_count, cap, HD), bf16),
             pltpu.VMEM((z_count, y_count, cap, HD), bf16),
-            pltpu.VMEM((y_count, cap, WIDE), bf16),
             pltpu.VMEM((z_count, y_count, cap, HD), bf16),
             pltpu.VMEM((z_count, y_count, cap, HD), bf16),
             pltpu.SemaphoreType.DMA((5,)),
             pltpu.SemaphoreType.DMA((3,)),
-            pltpu.VMEM((GROUP, most + cap, HD), f32),
-            pltpu.VMEM((GROUP, most + cap, HD), f32),
-            pltpu.VMEM((most + cap, HD), f32),
             pltpu.VMEM((row_blocks + 1, lanes, HD), bf16),
             pltpu.VMEM((row_blocks + 1, lanes, HD), bf16),
             pltpu.VMEM((row_blocks + 1, 1, lanes), f32),
@@ -611,9 +566,9 @@
 
 def scatter_kernel(
     y_count, z_count, dp_count,
-    dq_in, dk_hbm, dv_hbm, part,
-    dq_out, dk_out, dv_out, router_out, dk_in, dv_in,
-    held, fin, dp_held, y_held, z_held, dp_sum, y_sum, dq_own,
+    dq_hbm, dk_hbm, dv_hbm, part,
+    dq_out, dk_out, dv_out, router_out, dq_in, dk_in, dv_in,
+    held, fin, dp_held, y_held, z_held, dp_sum, y_sum, dq_v,
     own_sem, q_send, q_recv, ring_send, ring_recv, fin_send, fin_recv, r_send, r_recv,
 ):
     y, z = place(z_count)
@@ -640,21 +595,22 @@
     own_in = [
         pltpu.make_async_copy(dk_hbm, dk_in, own_sem.at[1]),
         pltpu.make_async_copy(dv_hbm, dv_in, own_sem.at[2]),
-        pltpu.make_async_copy(dq_in.at[y], dq_own, own_sem.at[0]),
+        pltpu.make_async_copy(dq_hbm, dq_in, own_sem.at[0]),
     ]
     for copy in own_in:
         copy.start()
+    for copy in own_in[:2]:
+        copy.wait()
     pl.semaphore_wait(pltpu.get_barrier_semaphore(), len(peers))
 
     plan = ring_plan(z_count)
     mine = (dk_in, dv_in)
-    apart = (dk_hbm, dv_hbm)
 
     def ring_copy(lane, step):
         array, way, steps = plan[lane]
         block = (z + way * (steps - step) + z_count) % z_count
         there = at(y, right if way == 1 else left)
-        source = apart[array].at[block] if step == 0 else held.at[lane, step - 1]
+        source = mine[array].at[block] if step == 0 else held.at[lane, step - 1]
         return remote(source, held.at[lane, step], ring_send.at[lane, step], ring_recv.at[lane, step], there)
 
     def forward(step):
@@ -669,13 +625,23 @@
                 ring_copy(lane, step).start()
 
     forward(0)
+    own_in[2].wait()
+    block_rows = dq_in.shape[2] // GROUP
+    halves = dq_v.shape[1] // block_rows
+
+    def turn_rows(b, carry):
+        rows = pl.ds(pl.multiple_of(b % halves * block_rows, block_rows), block_rows)
+        turned = (dq_in[b].T * (1.0 / math.sqrt(HD))).astype(bf16)
+        for h in range(GROUP):
+            dq_v[b // halves, rows, h * HD : (h + 1) * HD] = turned[h * block_rows : (h + 1) * block_rows, :]
+        return carry
+
+    lax.fori_loop(0, dq_in.shape[0], turn_rows, 0)
     sends = []
     for i, other in enumerate(y_peers):
-        sends.append(remote(dq_in.at[other], wide(dq_out, y), q_send.at[i], q_recv.at[i], at(other, z)))
+        sends.append(remote(dq_v.at[other], wide(dq_out, y), q_send.at[i], q_recv.at[i], at(other, z)))
         sends[-1].start()
-    for copy in own_in:
-        copy.wait()
-    own = [pltpu.make_async_copy(dq_own, wide(dq_out, y), own_sem.at[0])]
+    own = [pltpu.make_async_copy(dq_v.at[y], wide(dq_out, y), own_sem.at[0])]
     own[0].start()
 
     def share(first, source_of, held_ref, peers_there, me):
@@ -709,7 +675,13 @@
         copy.wait()
     for other in z_peers:
         total = total + z_held[other]
-    router_out[...] = total
+    first = lax.axis_index("seq") * router_out.shape[1]
+    lane = lax.broadcasted_iota(jnp.int32, (1, HD), 1)
+    here = jnp.zeros((1, HD), f32)
+    for row in range(total.shape[0]):
+        turned = pltpu.roll(total[row : row + 1, :], (HD - first % HD) % HD, 1)
+        here = jnp.where((first + lane) // HD == row, turned, here)
+    router_out[...] = here[:, : router_out.shape[1]]
 
     ends = []
     for array, target in ((0, dk_out), (1, dv_out)):
@@ -742,7 +714,8 @@
 
 
 def scatter(y_count, z_count, dp_count, dq_in, dk_in, dv_in, part):
-    cap = dq_in.shape[1]
+    share = part.shape[1] * HD // (y_count * z_count)
+    cap = dk_in.shape[2]
     longer = z_count // 2
     small = part.shape[1:]
     anywhere = pl.BlockSpec(memory_space=pl.ANY)
@@ -756,11 +729,12 @@
             shape((cap, HEADS * HD), bf16),
             shape((cap, KV * HD), bf16),
             shape((cap, KV * HD), bf16),
-            shape(small, f32),
+            shape((1, share), f32),
         ),
         in_specs=[anywhere, anywhere, anywhere, vmem],
         out_specs=(anywhere, anywhere, anywhere, vmem),
         scratch_shapes=[
+            pltpu.VMEM(dq_in.shape, f32),
             pltpu.VMEM((z_count, y_count, cap, HD), bf16),
             pltpu.VMEM((z_count, y_count, cap, HD), bf16),
             pltpu.VMEM((4, longer, y_count, cap, HD), bf16),
@@ -770,7 +744,7 @@
             pltpu.VMEM((z_count,) + small, f32),
             pltpu.VMEM(small, f32),
             pltpu.VMEM(small, f32),
-            pltpu.VMEM((cap, WIDE), bf16),
+            pltpu.VMEM((y_count, cap, WIDE), bf16),
             pltpu.SemaphoreType.DMA((3,)),
             pltpu.SemaphoreType.DMA((y_count - 1,)),
             pltpu.SemaphoreType.DMA((y_count - 1,)),
@@ -789,25 +763,18 @@
 
 
 def result_kernel(
-    dq_in, dk_in, dv_in, router, dq_out, dk_out, dv_out, share, dq_v, dk_v, dv_v, in_sem, out_sem
+    dq_in, dk_in, dv_in, share_in, dq_out, dk_out, dv_out, share_out, dq_v, dk_v, dv_v, share_v, in_sem, out_sem
 ):
     moves = []
     rows = dq_v.shape[1]
     for i in range(dq_v.shape[0]):
         part = pl.ds(i * rows, rows)
         moves.append((dq_in.at[part], dq_v.at[i], dq_out.at[part]))
-    moves += [(dk_in, dk_v, dk_out), (dv_in, dv_v, dv_out)]
+    moves += [(dk_in, dk_v, dk_out), (dv_in, dv_v, dv_out), (share_in, share_v, share_out)]
     loads = [pltpu.make_async_copy(a, b, in_sem.at[i]) for i, (a, b, _) in enumerate(moves)]
     stores = [pltpu.make_async_copy(b, c, out_sem.at[i]) for i, (_, b, c) in enumerate(moves)]
     for load in loads:
         load.start()
-    first = lax.axis_index("seq") * share.shape[1]
-    lane = lax.broadcasted_iota(jnp.int32, (1, HD), 1)
-    here = jnp.zeros((1, HD), jnp.float32)
-    for row in range(router.shape[0]):
-        turned = pltpu.roll(router[row : row + 1, :], (HD - first % HD) % HD, 1)
-        here = jnp.where((first + lane) // HD == row, turned, here)
-    share[...] = here[:, : share.shape[1]]
     for load, store in zip(loads, stores):
         load.wait()
         store.start()
@@ -815,41 +782,39 @@
         store.wait()
 
 
-def results(share, dq, dk, dv, router):
-    vmem = pl.BlockSpec(memory_space=pltpu.VMEM)
+def results(dq, dk, dv, share):
     anywhere = pl.BlockSpec(memory_space=pl.ANY)
     pieces = 4
     shape = jax.ShapeDtypeStruct
     return pl.pallas_call(
         result_kernel,
-        out_shape=tuple(shape(x.shape, x.dtype) for x in (dq, dk, dv)) + (shape((1, share), jnp.float32),),
-        in_specs=[anywhere] * 3 + [vmem],
-        out_specs=(anywhere,) * 3 + (vmem,),
+        out_shape=tuple(shape(x.shape, x.dtype) for x in (dq, dk, dv, share)),
+        in_specs=[anywhere] * 4,
+        out_specs=(anywhere,) * 4,
         scratch_shapes=[
             pltpu.VMEM((pieces, dq.shape[0] // pieces, dq.shape[1]), dq.dtype),
             pltpu.VMEM(dk.shape, dk.dtype),
             pltpu.VMEM(dv.shape, dv.dtype),
-            pltpu.SemaphoreType.DMA((pieces + 2,)),
-            pltpu.SemaphoreType.DMA((pieces + 2,)),
+            pltpu.VMEM(share.shape, share.dtype),
+            pltpu.SemaphoreType.DMA((pieces + 3,)),
+            pltpu.SemaphoreType.DMA((pieces + 3,)),
         ],
         compiler_params=pltpu.CompilerParams(vmem_limit_bytes=63 * MIB),
         name="results",
-    )(dq, dk, dv, router)
+    )(dq, dk, dv, share)
 
 
 def on_device(tokens, router_weight, routes, counts, query, key_in, value_in, attn_out, grad_out):
     y_count = KV
     z_count = lax.axis_size("seq") // y_count
     dp_count = lax.axis_size("dp")
-    width = tokens.shape[2]
     q_all, do_all, de_all, k_all, v_all, c_all, part = gather(
         y_count, z_count, dp_count, tokens[0], router_weight[None], routes, counts,
         query[0], key_in[0], value_in[0], attn_out[0], grad_out[0],
     )
     dq, dk, dv = attention(y_count, z_count, c_all, q_all, do_all, de_all, k_all, v_all)
     dq, dk, dv, router = scatter(y_count, z_count, dp_count, dq, dk, dv, part)
-    share = width // (dp_count * y_count * z_count)
-    dq, dk, dv, router = results(share, dq, dk, dv, router)
+    dq, dk, dv, router = results(dq, dk, dv, router)
     return (dq[None], dk[None], dv[None], router[0])
 
 

time: 102 us -> 103 us (level)
    pallas_call x1, Pallas kernels: 16 us -> 17.9 us  [attention(): pl.pallas_call(functools.partial(attention_kernel, y_count, z_count, bloc...]
    pallas_call x1, Pallas kernels: 3.29 us -> 2.12 us  [results(): pl.pallas_call(result_kernel, out_shape=tuple((shape(x.shape, x.dtype) fo...]
where the time goes in v5:
time: 103 us; the launch traced here: 102 us
  Pallas kernels  101 us (98%)
  between operations  1.3 us (1%)
    pallas_call x1, Pallas kernels, scatter(): pl.pallas_call(functools.partial(scatter_kernel, y_count, z_count, dp_cou...  42.9 us
    pallas_call x1, Pallas kernels, gather(): pl.pallas_call(functools.partial(gather_kernel, y_count, z_count, chunks)...  37.7 us
    pallas_call x1, Pallas kernels, attention(): pl.pallas_call(functools.partial(attention_kernel, y_count, z_count, bloc...  17.9 us
    pallas_call x1, Pallas kernels, results(): pl.pallas_call(result_kernel, out_shape=tuple((shape(x.shape, x.dtype) fo...  2.12 us

profile of v5, /device:TPU:6, one launch (start us, length us, event | category | flops | bytes accessed | tf_op | source)
XLA Modules:
  0.0 101.9 jit_solution(6931475089981821902)
XLA Ops:
  1.3 37.7 %gather.1 = (bf16[4,128,1024]{2,1,0:T(8,128)(2,1)}, bf16[4,128,1024]{2,1,0:T(8,128)(2,1)}, f32[4,8,128]{2,1,0:T(8,128)}, bf16[8,4,128,128]{3,2,1,0:T(8,128)(2,1)...) custom-call(bf16[512,5120]{1,0:T(8,128)(2,1)} %bitcast.11, ...), custom_call_target="tpu_custom_call" | custom-call | tf_op jit(solution)/shard_map/gather/pallas_call | solution.py:246
  39.0 17.9 %attention.1 = (f32[8,128,512]{2,1,0:T(8,128)}, bf16[8,4,128,128]{3,2,1,0:T(8,128)(2,1)}, bf16[8,4,128,128]{3,2,1,0:T(8,128)(2,1)}) custom-call(s32[8,4,1,128]{3,2,1,0:T(1,128)} %get-tuple-element.22.counts, bf16[4,128,1024]{2,1,0:T(8,128)(2,1)} %get-tuple-element.23.q_hbm, bf16[4,128,1024]{2,1,0:T(8,128)(2,1)} %get-tuple-element.24.do_hbm, ...), custom_call_target="tpu_custom_call" | custom-call | tf_op jit(solution)/shard_map/attention/pallas_call | solution.py:518
  56.9 42.9 %scatter.1 = (bf16[128,4096]{1,0:T(8,128)(2,1)}, bf16[128,512]{1,0:T(8,128)(2,1)}, bf16[128,512]{1,0:T(8,128)(2,1)}, f32[1,20]{1,0:T(1,128)}) custom-call(f32[8,128,512]{2,1,0:T(8,128)} %get-tuple-element.28.dq_hbm, bf16[8,4,128,128]{3,2,1,0:T(8,128)(2,1)} %get-tuple-element.29.dk_hbm, bf16[8,4,128,128]{3,2,1,0:T(8,128)(2,1)} %get-tuple-element.30.dv_hbm, ...), custom_call_target="tpu_custom_call" | custom-call | tf_op jit(solution)/shard_map/scatter/pallas_call | solution.py:726
  99.8 2.1 %results.1 = (bf16[128,4096]{1,0:T(8,128)(2,1)}, bf16[128,512]{1,0:T(8,128)(2,1)}, bf16[128,512]{1,0:T(8,128)(2,1)}, f32[1,20]{1,0:T(1,128)}) custom-call(bf16[128,4096]{1,0:T(8,128)(2,1)} %get-tuple-element.32.dq_in, bf16[128,512]{1,0:T(8,128)(2,1)} %get-tuple-element.33.dk_in, bf16[128,512]{1,0:T(8,128)(2,1)} %get-tuple-element.34.dv_in, ...), custom_call_target="tpu_custom_call" | custom-call | tf_op jit(solution)/shard_map/results/pallas_call | solution.py:789

commit v6 on v5

--- a/solution.py
+++ b/solution.py
@@ -398,14 +398,16 @@
 
     def grow(masked, n, slot):
         b, kb = pair_row[n], pair_key[n]
+        if masked:
+            lane = lax.broadcasted_iota(jnp.int32, (8, SUB_LANES), 1)
+            sublane = lax.broadcasted_iota(jnp.int32, (8, SUB_LANES), 0)
+            ahead = first_place(b) - kb * block_keys + lane % block_rows - sublane
         for part in range(lanes // SUB_LANES):
             cols = slice(part * SUB_LANES, (part + 1) * SUB_LANES)
             block = s_b[slot][:, cols] * power
             if masked:
-                lane = lax.broadcasted_iota(jnp.int32, (1, SUB_LANES), 1)
-                row_place = first_place(b) + lane % block_rows - kb * block_keys
-                key_place = lax.broadcasted_iota(jnp.int32, (block_keys, SUB_LANES), 0)
-                block = jnp.where(key_place <= row_place, block, NEGATIVE)
+                allowed = ahead[None] >= 8 * lax.broadcasted_iota(jnp.int32, (block_keys // 8, 8, SUB_LANES), 0)
+                block = jnp.where(allowed, block.reshape(block_keys // 8, 8, SUB_LANES), NEGATIVE)
             block = block.reshape(block_keys // 8, 8, SUB_LANES)
             before = best[b, :, cols]
             after = jnp.maximum(before, jnp.max(block, axis=0))
@@ -427,6 +429,17 @@
     for many in DEEP:
         lax.fori_loop(done // many, whole_pairs // many, functools.partial(some_scores, False, many), 0)
         done = whole_pairs // many * many
+    fours = jnp.maximum(pairs - done, 0) // 4
+
+    def four_scores(j, carry):
+        for more in range(4):
+            n = done + 4 * j + more
+            raw(n + 1, (more + 1) % 2)
+            grow(True, n, more % 2)
+        return carry
+
+    lax.fori_loop(0, fours, four_scores, 0)
+    done = done + 4 * fours
     lax.fori_loop(done // 2, (pairs + 1) // 2, functools.partial(some_scores, True, 2), 0)
 
     def finish_rows(b, carry):
@@ -480,27 +493,26 @@
     stores[0].start()
     slot = lax.broadcasted_iota(jnp.int32, (cap, 1), 0)
 
-    def widen_keys(b, carry):
-        rows = pl.ds(pl.multiple_of(b * block_keys, block_keys), block_keys)
-        k_f[rows, :] = dk_f[b] * root
-        v_f[rows, :] = dv_f[b]
-        return carry
-
-    lax.fori_loop(0, key_blocks, widen_keys, 0)
-
-    def unpack_keys(step, carry):
-        for more in range(4):
-            shard = step * 4 + more
-            zz, yy = shard % z_count, shard // z_count
-            rows = pl.ds(shard_start[shard], cap)
-            held = slot < count_of(shard)
-            dk_out[zz, yy] = jnp.where(held, k_f[rows, :], 0.0).astype(bf16)
-            dv_out[zz, yy] = jnp.where(held, v_f[rows, :], 0.0).astype(bf16)
-        return carry
-
-    lax.fori_loop(0, shard_count // 4, unpack_keys, 0)
-    for store in stores[1:]:
+    def unpack(total, scale, packed, target, store):
+        def widen(b, carry):
+            rows = pl.ds(pl.multiple_of(b * block_keys, block_keys), block_keys)
+            packed[rows, :] = total[b] * scale
+            return carry
+
+        def place_shards(step, carry):
+            for more in range(4):
+                shard = step * 4 + more
+                rows = packed[pl.ds(shard_start[shard], cap), :]
+                rows = jnp.where(slot < count_of(shard), rows, 0.0)
+                target[shard % z_count, shard // z_count] = rows.astype(bf16)
+            return carry
+
+        lax.fori_loop(0, key_blocks, widen, 0)
+        lax.fori_loop(0, shard_count // 4, place_shards, 0)
         store.start()
+
+    unpack(dk_f, root, k_f, dk_out, stores[1])
+    unpack(dv_f, 1.0, v_f, dv_out, stores[2])
     for store in stores:
         store.wait()
 
@@ -597,7 +609,7 @@
         pltpu.make_async_copy(dv_hbm, dv_in, own_sem.at[2]),
         pltpu.make_async_copy(dq_hbm, dq_in, own_sem.at[0]),
     ]
-    for copy in own_in:
+    for copy in own_in[:2]:
         copy.start()
     for copy in own_in[:2]:
         copy.wait()
@@ -625,6 +637,7 @@
                 ring_copy(lane, step).start()
 
     forward(0)
+    own_in[2].start()
     own_in[2].wait()
     block_rows = dq_in.shape[2] // GROUP
     halves = dq_v.shape[1] // block_rows

time: 103 us -> 99.9 us (0.970)
  Pallas kernels: 101 us -> 96.8 us
    pallas_call x1, Pallas kernels: 42.9 us -> 39.5 us  [scatter(): pl.pallas_call(functools.partial(scatter_kernel, y_count, z_count, dp_cou...]
where the time goes in v6:
time: 99.9 us; the launch traced here: 98.1 us
  Pallas kernels  96.8 us (97%)
  between operations  1.3 us (1%)
    pallas_call x1, Pallas kernels, scatter(): pl.pallas_call(functools.partial(scatter_kernel, y_count, z_count, dp_cou...  39.5 us
    pallas_call x1, Pallas kernels, gather(): pl.pallas_call(functools.partial(gather_kernel, y_count, z_count, chunks)...  37.7 us
    pallas_call x1, Pallas kernels, attention(): pl.pallas_call(functools.partial(attention_kernel, y_count, z_count, bloc...  17.5 us
    pallas_call x1, Pallas kernels, results(): pl.pallas_call(result_kernel, out_shape=tuple((shape(x.shape, x.dtype) fo...  2.12 us

profile of v6, /device:TPU:6, one launch (start us, length us, event | category | flops | bytes accessed | tf_op | source)
XLA Modules:
  0.0 98.1 jit_solution(14316900028005652673)
XLA Ops:
  1.3 37.7 %gather.1 = (bf16[4,128,1024]{2,1,0:T(8,128)(2,1)}, bf16[4,128,1024]{2,1,0:T(8,128)(2,1)}, f32[4,8,128]{2,1,0:T(8,128)}, bf16[8,4,128,128]{3,2,1,0:T(8,128)(2,1)...) custom-call(bf16[512,5120]{1,0:T(8,128)(2,1)} %bitcast.11, ...), custom_call_target="tpu_custom_call" | custom-call | tf_op jit(solution)/shard_map/gather/pallas_call | solution.py:246
  39.0 17.5 %attention.1 = (f32[8,128,512]{2,1,0:T(8,128)}, bf16[8,4,128,128]{3,2,1,0:T(8,128)(2,1)}, bf16[8,4,128,128]{3,2,1,0:T(8,128)(2,1)}) custom-call(s32[8,4,1,128]{3,2,1,0:T(1,128)} %get-tuple-element.22.counts, bf16[4,128,1024]{2,1,0:T(8,128)(2,1)} %get-tuple-element.23.q_hbm, bf16[4,128,1024]{2,1,0:T(8,128)(2,1)} %get-tuple-element.24.do_hbm, ...), custom_call_target="tpu_custom_call" | custom-call | tf_op jit(solution)/shard_map/attention/pallas_call | solution.py:530
  56.5 39.5 %scatter.1 = (bf16[128,4096]{1,0:T(8,128)(2,1)}, bf16[128,512]{1,0:T(8,128)(2,1)}, bf16[128,512]{1,0:T(8,128)(2,1)}, f32[1,20]{1,0:T(1,128)}) custom-call(f32[8,128,512]{2,1,0:T(8,128)} %get-tuple-element.28.dq_hbm, bf16[8,4,128,128]{3,2,1,0:T(8,128)(2,1)} %get-tuple-element.29.dk_hbm, bf16[8,4,128,128]{3,2,1,0:T(8,128)(2,1)} %get-tuple-element.30.dv_hbm, ...), custom_call_target="tpu_custom_call" | custom-call | tf_op jit(solution)/shard_map/scatter/pallas_call | solution.py:739
  96.0 2.1 %results.1 = (bf16[128,4096]{1,0:T(8,128)(2,1)}, bf16[128,512]{1,0:T(8,128)(2,1)}, bf16[128,512]{1,0:T(8,128)(2,1)}, f32[1,20]{1,0:T(1,128)}) custom-call(bf16[128,4096]{1,0:T(8,128)(2,1)} %get-tuple-element.32.dq_in, bf16[128,512]{1,0:T(8,128)(2,1)} %get-tuple-element.33.dk_in, bf16[128,512]{1,0:T(8,128)(2,1)} %get-tuple-element.34.dv_in, ...), custom_call_target="tpu_custom_call" | custom-call | tf_op jit(solution)/shard_map/results/pallas_call | solution.py:802
